TPU v7x, 256 devices: a whole 4x4x8 slice. The times are simulated.
256 devices in a mesh: shard: 64 (over z, x, core), sub: 4 (over y).
Axes of the slice: x: 4, y: 4, z: 8, core: 2. Of those that a mesh axis runs over, the one named last changes fastest.
Arguments:
- feats: bfloat16 [8192, 4096], P(('shard', 'sub')), may hold values from -24 to 24
- w_hidden: bfloat16 [4096, 4096], P(None, 'sub'), may hold values from -0.09375 to 0.09375
- w_embed: bfloat16 [4096, 256], P('sub'), may hold values from -0.09375 to 0.09375
- items: bfloat16 [262144, 256], P(('shard', 'sub')), may hold values from -0.5 to 0.5
- teacher: bfloat16 [65536, 128], P(('shard', 'sub')), may hold values from -6 to 6
- block_counts: int32 [256, 32], P(('shard', 'sub')), may hold values from 1 to 32, 256 in all within a row
- tail_rows: int32 [8192], P(('shard', 'sub')), may hold values from 1 to 128
- cand_owner: int32 [65536, 1], P(('shard', 'sub')), may hold values from 0 to 255; in each aligned block of 256 rows (0 to 255, 256 to 511, ...) at most 2 rows name the same one
- cand_block: int32 [65536], P(('shard', 'sub')), may hold values from 0 to 7
Outputs:
- grad_feats: float32 [8192, 4096], P(('shard', 'sub'))
- grad_hidden: float32 [4096, 4096], P('shard', 'sub')
- grad_embed: float32 [4096, 256], P('sub')
- grad_items: float32 [262144, 256], P(('shard', 'sub'))
Inputs may be any that keep to these rules, and one draw needn't show every extreme that they name: `block_counts`: each device's row sums to 256; one count in each row is exactly 32. `cand_owner`: among the rows of one device no owner appears more than 2 times; some owner appears exactly 2 times in some device's rows.
All inputs are finite; a program needn't handle non-finite values.
Results may differ from a plain program's by a relative error of at most 0.013.
Values may be sent and summed in bfloat16 or wider, within the bound.
A program may use at most 128 MiB of HBM per device.

v0:
```python
import jax
import jax.numpy as jnp
from jax import lax
from jax.sharding import PartitionSpec as P

BLK = 128
BLK_DEV = 8


eps_norm = 1e-06


def contract_first(left, right):
    return lax.dot_general(
        left, right, (((0,), (0,)), ((), ())), preferred_element_type=jnp.float32
    )


def contract_last(left, right):
    return lax.dot_general(
        left, right, (((1,), (1,)), ((), ())), preferred_element_type=jnp.float32
    )


def query_softmax(logits, valid_row, group_member, local_query):
    masked = jnp.where(valid_row, logits, -jnp.inf)
    slot_top = jnp.max(masked, axis=1)
    query_top = jnp.max(jnp.where(group_member, slot_top[None, :], -jnp.inf), axis=1)
    expo = jnp.where(valid_row, jnp.exp(logits - query_top[local_query][:, None]), 0.0)
    slot_total = jnp.sum(expo, axis=1)
    query_count_total = jnp.sum(jnp.where(group_member, slot_total[None, :], 0.0), axis=1)
    return expo / query_count_total[local_query][:, None]


def per_device(
    feats, w_hidden, w_embed, items, teacher, block_counts, tail_rows, cand_owner, cand_block
):
    n_shard = lax.axis_size("shard")
    n_sub = lax.axis_size("sub")
    q_dev = feats.shape[0]
    emb_width = w_embed.shape[1]
    gathered = lax.all_gather(feats, "sub", axis=0, tiled=True)
    preact = jnp.dot(gathered, w_hidden, preferred_element_type=jnp.float32)
    hidden = jax.nn.silu(preact).astype(jnp.bfloat16)
    row_block = hidden
    emb_raw = lax.psum_scatter(
        jnp.dot(row_block, w_embed, preferred_element_type=jnp.float32),
        "sub",
        scatter_dimension=0,
        tiled=True,
    )
    inv_rms = lax.rsqrt(jnp.mean(emb_raw * emb_raw, axis=1, keepdims=True) + eps_norm)
    query_emb = (emb_raw * inv_rms).astype(jnp.bfloat16)
    slot_count = cand_owner.shape[0]
    device_count = n_shard * n_sub
    capacity = max(2, (2 * slot_count + device_count - 1) // device_count)
    buffer_rows = device_count * capacity
    counts_row = block_counts[0]
    seg_ends = jnp.cumsum(counts_row)
    slot_pos = jnp.arange(slot_count, dtype=jnp.int32)
    local_query = jnp.sum((slot_pos[:, None] >= seg_ends[None, :]).astype(jnp.int32), axis=1)
    group_member = jnp.arange(q_dev, dtype=jnp.int32)[:, None] == local_query[None, :]
    is_last = slot_pos == seg_ends[local_query] - 1
    tail_fill = tail_rows[local_query]
    row_pos = jnp.arange(BLK, dtype=jnp.int32)
    valid_row = jnp.logical_or(
        jnp.logical_not(is_last)[:, None], row_pos[None, :] < tail_fill[:, None]
    )
    owner_dev = cand_owner[:, 0]
    earlier = jnp.logical_and(
        owner_dev[None, :] == owner_dev[:, None], slot_pos[None, :] < slot_pos[:, None]
    )
    rank_owner = jnp.sum(earlier.astype(jnp.int32), axis=1)
    dest_row = owner_dev * capacity + rank_owner
    query_slot = query_emb[local_query]
    query_buf = jnp.zeros((buffer_rows, emb_width), jnp.bfloat16).at[dest_row].set(query_slot)
    query_buf = query_buf.reshape(n_shard, n_sub, capacity, emb_width)
    index_buf = jnp.full((buffer_rows,), -1, jnp.int32).at[dest_row].set(cand_block)
    index_buf = index_buf.reshape(n_shard, n_sub, capacity)
    query_in, index_in = (
        lax.all_to_all(
            lax.all_to_all(query_buf, "shard", split_axis=0, concat_axis=0, tiled=True),
            "sub",
            split_axis=1,
            concat_axis=1,
            tiled=True,
        ),
        lax.all_to_all(
            lax.all_to_all(index_buf, "shard", split_axis=0, concat_axis=0, tiled=True),
            "sub",
            split_axis=1,
            concat_axis=1,
            tiled=True,
        ),
    )
    flat_query = query_in.reshape(buffer_rows, emb_width)
    flat_index = index_in.reshape(buffer_rows)
    pick_block = flat_index[:, None] == jnp.arange(BLK_DEV, dtype=jnp.int32)[None, :]
    all_scores = contract_last(flat_query, items).reshape(buffer_rows, BLK_DEV, BLK)
    owner_scores = jnp.sum(jnp.where(pick_block[:, :, None], all_scores, 0.0), axis=1)
    returned = lax.all_to_all(
        lax.all_to_all(
            owner_scores.reshape(n_shard, n_sub, capacity, BLK),
            "shard",
            split_axis=0,
            concat_axis=0,
            tiled=True,
        ),
        "sub",
        split_axis=1,
        concat_axis=1,
        tiled=True,
    )
    scores = returned.reshape(buffer_rows, BLK)[dest_row]
    student_p = query_softmax(scores, valid_row, group_member, local_query)
    teacher_p = query_softmax(teacher.astype(jnp.float32), valid_row, group_member, local_query)
    n_cand = ((counts_row - 1) * BLK + tail_rows).astype(jnp.float32)
    dlogit = jnp.where(valid_row, n_cand[local_query][:, None] * (student_p - teacher_p), 0.0)
    dlogit_buf = jnp.zeros((buffer_rows, BLK), jnp.float32).at[dest_row].set(dlogit)
    dlogit_buf = dlogit_buf.reshape(n_shard, n_sub, capacity, BLK)
    dlogit_in = lax.all_to_all(
        lax.all_to_all(dlogit_buf, "shard", split_axis=0, concat_axis=0, tiled=True),
        "sub",
        split_axis=1,
        concat_axis=1,
        tiled=True,
    )
    spread = jnp.where(pick_block[:, :, None], dlogit_in.reshape(buffer_rows, 1, BLK), 0.0)
    spread = spread.reshape(buffer_rows, BLK_DEV * BLK)
    grad_items = lax.dot_general(
        spread,
        flat_query.astype(jnp.float32),
        (((0,), (0,)), ((), ())),
        precision=lax.Precision.HIGHEST,
        preferred_element_type=jnp.float32,
    )
    owner_dq = jnp.dot(
        spread,
        items.astype(jnp.float32),
        precision=lax.Precision.HIGHEST,
        preferred_element_type=jnp.float32,
    )
    dq_back = lax.all_to_all(
        lax.all_to_all(
            owner_dq.reshape(n_shard, n_sub, capacity, emb_width),
            "shard",
            split_axis=0,
            concat_axis=0,
            tiled=True,
        ),
        "sub",
        split_axis=1,
        concat_axis=1,
        tiled=True,
    )
    query_grad_slot = dq_back.reshape(buffer_rows, emb_width)[dest_row]
    query_gradient = jnp.dot(
        group_member.astype(jnp.float32), query_grad_slot, precision=lax.Precision.HIGHEST
    )
    grad_emb = (
        inv_rms
        * (
            query_gradient
            - emb_raw
            * inv_rms
            * inv_rms
            * jnp.mean(query_gradient * emb_raw, axis=1, keepdims=True)
        )
    ).astype(jnp.bfloat16)
    grad_emb_all = lax.all_gather(grad_emb, "sub", axis=0, tiled=True)
    embed_term_local = contract_first(hidden, grad_emb_all)
    grad_embed = lax.psum(embed_term_local, "shard")
    dhidden = contract_last(grad_emb_all, w_embed)
    sigmoid_pre = jax.nn.sigmoid(preact)
    preact_gradient = (dhidden * sigmoid_pre * (1.0 + preact * (1.0 - sigmoid_pre))).astype(
        jnp.bfloat16
    )
    grad_hidden = lax.psum_scatter(
        contract_first(gathered, preact_gradient), "shard", scatter_dimension=0, tiled=True
    )
    row_block = preact_gradient
    grad_feats = lax.psum_scatter(
        contract_last(row_block, w_hidden), "sub", scatter_dimension=0, tiled=True
    )
    return (grad_feats, grad_hidden, grad_embed, grad_items)


def solution(mesh):
    placed = (
        P(("shard", "sub"), None),
        P(None, "sub"),
        P("sub", None),
        P(("shard", "sub"), None),
        P(("shard", "sub"), None),
        P(("shard", "sub"), None),
        P(("shard", "sub")),
        P(("shard", "sub"), None),
        P(("shard", "sub")),
    )
    return jax.shard_map(
        per_device,
        mesh=mesh,
        in_specs=placed,
        out_specs=(
            P(("shard", "sub"), None),
            P("shard", "sub"),
            P("sub", None),
            P(("shard", "sub"), None),
        ),
        check_vma=False,
    )
```

profile of v0, /device:TPU:1, one launch (start us, length us, event | category | flops | bytes accessed | tf_op | source)
XLA Modules:
  0.0 779.6 jit_solution(1002184609193983950)
XLA Ops:
  12.4 13.0 %all-to-all-start = ((s32[64,4,2]{1,2,0:T(2,128)}), s32[64,4,2]{1,2,0:T(2,128)S(1)}, u32[]{:S(2)}, u32[]{:S(2)}) async-start(s32[64,4,2]{1,2,0:T(2,128)} %copy.65), calls=%async_computation.1 | async-start | bytes 131072 | tf_op jit(solution)/shard_map/all_to_all | solution.py:89
  26.5 12.8 %all-gather.2.cloned.1.call-done = bf16[128,4096]{1,0:T(8,128)(2,1)} async-done(((bf16[32,4096]{1,0:T(8,128)(2,1)}), bf16[128,4096]{1,0:T(8,128)(2,1)}) %all-gather.2.cloned.1.call-update) | async-done | bytes 1048592 | tf_op jit(solution)/shard_map/all_gather | solution.py:42
  51.5 17.4 %reduce-scatter.6.cloned.1.call-done = f32[32,256]{1,0:T(8,128)} async-done(((f32[128,256]{1,0:T(8,128)}), f32[32,256]{1,0:T(8,128)}) %reduce-scatter.6.cloned.1.call-update) | async-done | bytes 32784 | tf_op jit(solution)/shard_map/reduce_scatter | solution.py:46
  73.6 12.9 %all-to-all-start.2 = ((bf16[64,4,2,256]{3,2,1,0:T(2,128)(2,1)}), bf16[64,4,2,256]{3,2,1,0:T(2,128)(2,1)S(1)}, u32[]{:S(2)}, u32[]{:S(2)}) async-start(bf16[64,4,2,256]{3,2,1,0:T(2,128)(2,1)} %reshape.153), calls=%async_computation.3 | async-start | bytes 524288 | tf_op jit(solution)/shard_map/all_to_all | solution.py:82
  91.5 8.1 %all-to-all-done.2 = bf16[64,4,2,256]{3,2,1,0:T(2,128)(2,1)S(1)} async-done(((bf16[64,4,2,256]{3,2,1,0:T(2,128)(2,1)}), bf16[64,4,2,256]{3,2,1,0:T(2,128)(2,1)S(1)}, u32[]{:S(2)}, u32[]{:S(2)}) %all-to-all-start.2) | async-done | bytes 262176 | tf_op jit(solution)/shard_map/all_to_all | solution.py:82
  104.0 6.5 all-to-all-done.3
  117.7 19.9 %select_select_fusion.4 = (f32[256]{0:T(256)S(1)}, pred[256]{0:T(512)(128)(4,1)S(1)}, pred[256]{0:T(512)(128)(4,1)S(1)}, pred[256]{0:T(512)(128)(4,1)S(1)}, pred...) fusion(f32[]{:T(128)} %bitcast.71, f32[]{:T(128)} %bitcast.72, ...), kind=kLoop, calls=%fused_computation.72 | loop fusion | flops 15872 | bytes 10112 | tf_op jit(solution)/shard_map/gather | solution.py:118
  137.6 20.1 %select_select_fusion.5 = s32[256]{0:T(256)S(1)} fusion(pred[256]{0:T(512)(128)(4,1)S(1)} %get-tuple-element.67, pred[256]{0:T(512)(128)(4,1)S(1)} %get-tuple-element.66, pred[256]{0:T(512)(128)(4,1)S(1)} %get-tuple-element.65, pred[256]{0:T(512)(128)(4,1)S(1)} %get-tuple-element.64, pred[256]{0:T(512)(128)(4,1)S(1)} %get-tuple-element.63, ...), kind=kLoop, calls=%fused_computation.73 | loop fusion | flops 7936 | bytes 9088 | tf_op jit(solution)/shard_map/gather | solution.py:64
  162.1 19.8 %compare_not_fusion = pred[256]{0:T(512)(128)(4,1)S(1)} fusion(pred[256]{0:T(512)(128)(4,1)S(1)} %get-tuple-element.67, pred[256]{0:T(512)(128)(4,1)S(1)} %get-tuple-element.66, pred[256]{0:T(512)(128)(4,1)S(1)} %get-tuple-element.65, pred[256]{0:T(512)(128)(4,1)S(1)} %get-tuple-element.64, pred[256]{0:T(512)(128)(4,1)S(1)} %get-tuple-element.63, ...), kind=kLoop, calls=%fused_computation.67 | loop fusion | flops 8704 | bytes 8320 | tf_op jit(solution)/shard_map/not | solution.py:67
  186.0 19.8 %select_select_fusion.1 = f32[256]{0:T(256)S(1)} fusion(pred[256]{0:T(512)(128)(4,1)S(1)} %get-tuple-element.67, pred[256]{0:T(512)(128)(4,1)S(1)} %get-tuple-element.66, pred[256]{0:T(512)(128)(4,1)S(1)} %get-tuple-element.65, pred[256]{0:T(512)(128)(4,1)S(1)} %get-tuple-element.64, pred[256]{0:T(512)(128)(4,1)S(1)} %get-tuple-element.63, ...), kind=kLoop, calls=%fused_computation.69 | loop fusion | flops 7936 | bytes 9088 | tf_op jit(solution)/shard_map/gather | solution.py:29
  205.8 20.1 %select_select_fusion.3 = f32[256]{0:T(256)S(1)} fusion(pred[256]{0:T(512)(128)(4,1)S(1)} %get-tuple-element.67, pred[256]{0:T(512)(128)(4,1)S(1)} %get-tuple-element.66, pred[256]{0:T(512)(128)(4,1)S(1)} %get-tuple-element.65, pred[256]{0:T(512)(128)(4,1)S(1)} %get-tuple-element.64, pred[256]{0:T(512)(128)(4,1)S(1)} %get-tuple-element.63, ...), kind=kLoop, calls=%fused_computation.71 | loop fusion | flops 7936 | bytes 9088 | tf_op jit(solution)/shard_map/gather | solution.py:29
  229.3 20.1 %select_select_fusion = f32[256]{0:T(256)S(1)} fusion(pred[256]{0:T(512)(128)(4,1)S(1)} %get-tuple-element.67, pred[256]{0:T(512)(128)(4,1)S(1)} %get-tuple-element.66, pred[256]{0:T(512)(128)(4,1)S(1)} %get-tuple-element.65, pred[256]{0:T(512)(128)(4,1)S(1)} %get-tuple-element.64, pred[256]{0:T(512)(128)(4,1)S(1)} %get-tuple-element.63, ...), kind=kLoop, calls=%fused_computation.68 | loop fusion | flops 7936 | bytes 9088 | tf_op jit(solution)/shard_map/gather | solution.py:32
  249.4 19.8 %select_select_fusion.2 = f32[256]{0:T(256)S(1)} fusion(pred[256]{0:T(512)(128)(4,1)S(1)} %get-tuple-element.67, pred[256]{0:T(512)(128)(4,1)S(1)} %get-tuple-element.66, pred[256]{0:T(512)(128)(4,1)S(1)} %get-tuple-element.65, pred[256]{0:T(512)(128)(4,1)S(1)} %get-tuple-element.64, pred[256]{0:T(512)(128)(4,1)S(1)} %get-tuple-element.63, ...), kind=kLoop, calls=%fused_computation.70 | loop fusion | flops 7936 | bytes 9088 | tf_op jit(solution)/shard_map/gather | solution.py:32
  270.7 23.3 %all_to_all.50 = f32[64,4,2,128]{3,2,1,0:T(2,128)S(1)} all-to-all(f32[64,4,2,128]{3,2,1,0:T(2,128)S(1)} %bitcast.274), channel_id=1, replica_groups=mesh['shard'=64,'sub'=4] {'shard'}, dimensions={0} | all-to-all | bytes 524288 | tf_op jit(solution)/shard_map/all_to_all | solution.py:122
  294.1 10.3 %all_to_all.51 = f32[64,4,2,128]{3,2,0,1:T(2,128)S(1)} all-to-all(f32[64,4,2,128]{3,2,0,1:T(2,128)S(1)} %copy.72), channel_id=1, replica_groups=mesh['shard'=64,'sub'=4] {'sub'}, dimensions={1} | all-to-all | bytes 524288 | tf_op jit(solution)/shard_map/all_to_all | solution.py:121
  315.1 23.1 %all_to_all.52 = f32[64,4,2,256]{3,2,1,0:T(2,128)S(1)} all-to-all(f32[64,4,2,256]{3,2,1,0:T(2,128)S(1)} %copy.76), channel_id=1, replica_groups=mesh['shard'=64,'sub'=4] {'shard'}, dimensions={0} | all-to-all | bytes 1048576 | tf_op jit(solution)/shard_map/all_to_all | solution.py:144
  338.4 11.6 %all_to_all.53 = f32[64,4,2,256]{3,2,0,1:T(2,128)S(1)} all-to-all(f32[64,4,2,256]{3,2,0,1:T(2,128)S(1)} %copy.77), channel_id=1, replica_groups=mesh['shard'=64,'sub'=4] {'sub'}, dimensions={1} | all-to-all | bytes 1048576 | tf_op jit(solution)/shard_map/all_to_all | solution.py:143
  351.9 9.1 %all_gather.7 = bf16[128,256]{1,0:T(8,128)(2,1)S(1)} all-gather(bf16[32,256]{1,0:T(8,128)(2,1)S(1)} %multiply_convert_fusion.1), channel_id=1, replica_groups=mesh['shard'=64,'sub'=4] {'sub'}, dimensions={0}, use_global_device_ids=true | all-gather | bytes 81920 | tf_op jit(solution)/shard_map/all_gather | solution.py:170
  363.9 7.6 fusion.52
  371.6 9.3 %convolution_bitcast_fusion = f32[4096,1024]{0,1:T(8,128)} fusion(bf16[128,1024]{1,0:T(8,128)(2,1)S(1)} %fusion.3, bf16[128,4096]{1,0:T(8,128)(2,1)} %all-gather.2.cloned.1.call-done), kind=kOutput, calls=%fused_computation.6 | convolution fusion | flops 1073741824 | bytes 18087936 | tf_op jit(solution)/shard_map/dot_general | solution.py:14
  380.9 17.5 %copy.82 = f32[4096,1024]{1,0:T(8,128)} copy(f32[4096,1024]{0,1:T(8,128)} %convolution_bitcast_fusion) | data formatting | bytes 33554432
  404.1 141.6 %all-reduce.2.cloned.1.call-done = f32[1024,256]{1,0:T(8,128)} async-done(((f32[1024,256]{1,0:T(8,128)}), f32[1024,256]{1,0:T(8,128)}) %all-reduce.2.cloned.1.call-update) | async-done | bytes 1048592 | tf_op jit(solution)/shard_map/psum | solution.py:172
  545.7 34.5 %reduce-scatter.8.cloned.1.call-done = f32[32,4096]{1,0:T(8,128)} async-done(((f32[128,4096]{1,0:T(8,128)}), f32[32,4096]{1,0:T(8,128)}) %reduce-scatter.8.cloned.1.call-update) | async-done | bytes 524304 | tf_op jit(solution)/shard_map/reduce_scatter | solution.py:182
  580.2 190.6 %reduce-scatter.10.cloned.1.call-done = f32[64,1024]{1,0:T(8,128)} async-done(((f32[4096,1024]{1,0:T(8,128)}), f32[64,1024]{1,0:T(8,128)}) %reduce-scatter.10.cloned.1.call-update) | async-done | bytes 262160
  (110 shorter events, 76.7 us)
Async XLA Ops:
  7.2 103.6 %copy-start = (bf16[1024,256]{1,0:T(8,128)(2,1)S(1)}, bf16[1024,256]{1,0:T(8,128)(2,1)}, u32[]{:S(2)}) copy-start(bf16[1024,256]{1,0:T(8,128)(2,1)} %param.12) | copy-start | bytes 1572868
  7.2 32.1 %all-gather.2.cloned.1.call-start = ((), (), s32[]{:S(2)}) async-start(), calls=%async_computation.13 | async-start | bytes 1310720 | tf_op jit(solution)/shard_map/all_gather | solution.py:42
  12.4 35.1 %all-to-all-start = ((s32[64,4,2]{1,2,0:T(2,128)}), s32[64,4,2]{1,2,0:T(2,128)S(1)}, u32[]{:S(2)}, u32[]{:S(2)}) async-start(s32[64,4,2]{1,2,0:T(2,128)} %copy.65), calls=%async_computation.1 | async-start | bytes 131072 | tf_op jit(solution)/shard_map/all_to_all | solution.py:89
  25.4 43.5 %reduce-scatter.6.cloned.1.call-start = ((), (), s32[]{:S(2)}) async-start(), calls=%async_computation.14 | async-start | bytes 163840 | tf_op jit(solution)/shard_map/reduce_scatter | solution.py:46
  26.5 19.3 %copy-start.5 = (bf16[1024,256]{1,0:T(8,128)(2,1)S(1)}, bf16[1024,256]{1,0:T(8,128)(2,1)}, u32[]{:S(2)}) copy-start(bf16[1024,256]{1,0:T(8,128)(2,1)} %param.11) | copy-start | bytes 1572868
  26.5 20.2 %copy-start.7 = (s32[32]{0:T(128)S(1)}, s32[32]{0:T(128)}, u32[]{:S(2)}) copy-start(s32[32]{0:T(128)} %param.15) | copy-start | bytes 388
  26.5 20.2 %copy-start.8 = (s32[1,32]{1,0:T(1,128)S(1)}, s32[1,32]{1,0:T(1,128)}, u32[]{:S(2)}) copy-start(s32[1,32]{1,0:T(1,128)} %param.14) | copy-start | bytes 388
  45.1 0.7 copy-start.2
  48.2 25.4 %all-to-all-start.1 = ((s32[4,1,128]{2,1,0:T(1,128)}), s32[4,1,128]{2,1,0:T(1,128)S(1)}, u32[]{:S(2)}, u32[]{:S(2)}) async-start(s32[4,1,128]{2,1,0:T(1,128)} %reshape.562), calls=%async_computation.2 | async-start | bytes 4096 | tf_op jit(solution)/shard_map/all_to_all | solution.py:88
  73.6 26.0 %all-to-all-start.2 = ((bf16[64,4,2,256]{3,2,1,0:T(2,128)(2,1)}), bf16[64,4,2,256]{3,2,1,0:T(2,128)(2,1)S(1)}, u32[]{:S(2)}, u32[]{:S(2)}) async-start(bf16[64,4,2,256]{3,2,1,0:T(2,128)(2,1)} %reshape.153), calls=%async_computation.3 | async-start | bytes 524288 | tf_op jit(solution)/shard_map/all_to_all | solution.py:82
  100.6 9.9 %all-to-all-start.3 = ((bf16[64,4,2,256]{3,2,0,1:T(2,128)(2,1)}), bf16[64,4,2,256]{3,2,0,1:T(2,128)(2,1)S(1)}, u32[]{:S(2)}, u32[]{:S(2)}) async-start(bf16[64,4,2,256]{3,2,0,1:T(2,128)(2,1)} %copy.68), calls=%async_computation.4 | async-start | bytes 524288 | tf_op jit(solution)/shard_map/all_to_all | solution.py:81
  112.3 70.5 %copy-start.4 = (bf16[256,128]{1,0:T(8,128)(2,1)S(1)}, bf16[256,128]{1,0:T(8,128)(2,1)}, u32[]{:S(2)}) copy-start(bf16[256,128]{1,0:T(8,128)(2,1)} %param.13) | copy-start | bytes 196612
  112.3 45.4 %all-to-all-start.4 = ((f32[64,4,2,128]{3,2,1,0:T(2,128)}), f32[64,4,2,128]{3,2,1,0:T(2,128)S(1)}, u32[]{:S(2)}, u32[]{:S(2)}) async-start(f32[64,4,2,128]{3,2,1,0:T(2,128)} %bitcast.104), calls=%async_computation.5 | async-start | bytes 524288 | tf_op jit(solution)/shard_map/all_to_all | solution.py:102
  158.4 23.5 %all-to-all-start.5 = ((f32[64,4,2,128]{3,2,0,1:T(2,128)}), f32[64,4,2,128]{3,2,0,1:T(2,128)S(1)}, u32[]{:S(2)}, u32[]{:S(2)}) async-start(f32[64,4,2,128]{3,2,0,1:T(2,128)} %copy.70), calls=%async_computation.6 | async-start | bytes 524288 | tf_op jit(solution)/shard_map/all_to_all | solution.py:101
  161.9 383.9 %all-reduce.2.cloned.1.call-start = ((), (), s32[]{:S(2)}) async-start(), calls=%async_computation.16 | async-start | bytes 2097152 | tf_op jit(solution)/shard_map/psum | solution.py:172
  350.0 1.5 copy-start.6
  350.5 10.5 %copy-start.3 = (bf16[128,1024]{1,0:T(8,128)(2,1)S(1)}, bf16[128,1024]{1,0:T(8,128)(2,1)}, u32[]{:S(2)}) copy-start(bf16[128,1024]{1,0:T(8,128)(2,1)} %copy-done.2) | copy-start | bytes 786436
  363.9 216.3 %reduce-scatter.8.cloned.1.call-start = ((), (), s32[]{:S(2)}) async-start(), calls=%async_computation.15 | async-start | bytes 2621440 | tf_op jit(solution)/shard_map/reduce_scatter | solution.py:182
  371.5 399.3 %reduce-scatter.10.cloned.1.call-start = ((), (), s32[]{:S(2)}) async-start(), calls=%async_computation.17 | async-start | bytes 17039360
  400.4 372.6 %copy-start.1 = (bf16[1024,256]{1,0:T(8,128)(2,1)S(1)}, bf16[1024,256]{1,0:T(8,128)(2,1)}, u32[]{:S(2)}) copy-start(bf16[1024,256]{1,0:T(8,128)(2,1)} %param.12) | copy-start | bytes 1572868
Sparse Core Ops, SparseCore 0:
  9.8 29.4 all-gather.1
  46.8 21.9 reduce-scatter.5
  364.0 181.6 all-reduce.1
  548.7 31.4 reduce-scatter.7
  585.8 184.9 reduce-scatter.9
where the time goes:
time: 786 us; the launch traced here: 780 us
  waiting for transfers between devices  412 us (52%)
  other arithmetic  147 us (19%)
  blocking collectives  77.3 us (10%)
  local copies, waits for them, and re-layouts  51.6 us (7%)
  starting transfers between devices  41.6 us (5%)
  matrix products  35.6 us (5%)
  between operations  14.2 us (2%)
    unnamed x6, waiting for transfers between devices  191 us
    psum x1, waiting for transfers between devices, per_device(): grad_embed = lax.psum(embed_term_local, 'shard')  142 us
    gather x2, other arithmetic, query_softmax(): return expo / query_count_total[local_query][:, None]  39.9 us
    gather x2, other arithmetic, query_softmax(): query_top[local_query][:, None]  39.9 us
    reduce_scatter x1, waiting for transfers between devices, per_device(): lax.psum_scatter(contract_last(row_block, w_hidden), 'sub', scatter_dimen...  34.5 us
    all_to_all x1, blocking collectives, per_device(): lax.all_to_all(dlogit_buf, 'shard', split_axis=0, concat_axis=0, tiled=True)  23.3 us
    all_to_all x1, blocking collectives, per_device(): lax.all_to_all(owner_dq.reshape(n_shard, n_sub, capacity, emb_width), 'sh...  23.1 us
    unnamed x22, local copies, waits for them, and re-layouts  21.3 us
  transfers between devices with their start and end apart: 11, of which 7 were waited for; matrix products, arithmetic and copies ran while one was open for 16% of the time, Pallas kernels for 0%

commit v1 on v0

v1 whole, which is shorter than its diff:
```python
import jax
import jax.numpy as jnp
from jax import lax
from jax.sharding import PartitionSpec as P

BLK = 128
BLK_DEV = 8
CAP = 2
EPS = 1e-06
HI = lax.Precision.HIGHEST
F32 = jnp.float32
BF16 = jnp.bfloat16


def dot(left, right, dims, precision=None):
    return lax.dot_general(
        left, right, ((dims[0], dims[1]), ((), ())), precision=precision, preferred_element_type=F32
    )


def nn(left, right, precision=None):
    return dot(left, right, ((1,), (0,)), precision)


def tn(left, right, precision=None):
    return dot(left, right, ((0,), (0,)), precision)


def nt(left, right, precision=None):
    return dot(left, right, ((1,), (1,)), precision)


def exchange(array):
    n_shard, n_sub = lax.axis_size("shard"), lax.axis_size("sub")
    shape = array.shape
    array = array.reshape((n_shard, n_sub, CAP) + shape[1:])
    array = lax.all_to_all(array, "shard", split_axis=0, concat_axis=0, tiled=True)
    array = lax.all_to_all(array, "sub", split_axis=1, concat_axis=1, tiled=True)
    return array.reshape(shape)


def per_device(
    feats, w_hidden, w_embed, items, teacher, block_counts, tail_rows, cand_owner, cand_block
):
    n_shard, n_sub = lax.axis_size("shard"), lax.axis_size("sub")
    q_dev = feats.shape[0]
    slots = cand_owner.shape[0]
    rows = n_shard * n_sub * CAP
    counts = block_counts[0]
    ends = jnp.cumsum(counts)
    pos = jnp.arange(slots, dtype=jnp.int32)[:, None]
    member = jnp.logical_and(pos < ends[None, :], pos >= (ends - counts)[None, :])
    used = jnp.where(pos == (ends - 1)[None, :], tail_rows[None, :], BLK)
    slot_used = jnp.sum(jnp.where(member, used, 0), axis=1, keepdims=True)
    valid = jnp.arange(BLK, dtype=jnp.int32)[None, :] < slot_used
    n_cand = ((counts - 1) * BLK + tail_rows).astype(F32)
    logit = teacher.astype(F32)
    top = jnp.max(jnp.where(valid, logit, -jnp.inf), axis=1, keepdims=True)
    query_top = jnp.max(jnp.where(member, top, -jnp.inf), axis=0, keepdims=True)
    slot_top = jnp.sum(jnp.where(member, query_top, 0.0), axis=1, keepdims=True)
    expo = jnp.where(valid, jnp.exp(logit - slot_top), 0.0)
    total = jnp.sum(
        jnp.where(member, jnp.sum(expo, axis=1, keepdims=True), 0.0), axis=0, keepdims=True
    )
    factor = jnp.sum(jnp.where(member, n_cand[None, :] / total, 0.0), axis=1, keepdims=True)
    teacher_n = expo * factor
    owner = cand_owner[:, 0]
    earlier = jnp.logical_and(owner[None, :] == owner[:, None], pos.T < pos)
    rank = jnp.sum(earlier.astype(jnp.int32), axis=1)
    dest = owner * CAP + rank
    place = jnp.arange(rows, dtype=jnp.int32)[:, None] == dest[None, :]
    info = jnp.sum(jnp.where(place, (cand_block * 256 + slot_used[:, 0])[None, :], 0), axis=1)
    member_row = nn(place.astype(BF16), member.astype(BF16))
    info_in = exchange(info)[:, None]
    teacher_in = exchange(nn(place.astype(F32), teacher_n, HI))
    block_in, used_in = info_in // 256, info_in % 256
    valid_in = jnp.arange(BLK, dtype=jnp.int32)[None, :] < used_in
    lane_block = jnp.arange(BLK_DEV * BLK, dtype=jnp.int32)[None, :] // BLK
    picked = lane_block == block_in

    def spread(values):
        return jnp.where(picked, jnp.tile(values, (1, BLK_DEV)), 0.0).astype(BF16)

    teacher_dq = exchange(nn(spread(teacher_in), items))
    query_teacher = tn(member_row, teacher_dq, HI)
    gathered = lax.all_gather(feats, "sub", axis=0, tiled=True)
    preact = nn(gathered, w_hidden)
    hidden = jax.nn.silu(preact).astype(BF16)
    emb_raw = lax.psum_scatter(nn(hidden, w_embed), "sub", scatter_dimension=0, tiled=True)
    inv_rms = lax.rsqrt(jnp.mean(emb_raw * emb_raw, axis=1, keepdims=True) + EPS)
    query_emb = (emb_raw * inv_rms).astype(BF16)
    query_in = exchange(nn(member_row.astype(BF16), query_emb).astype(BF16))
    every = nt(query_in, items)
    scores = jnp.zeros((rows, BLK), F32)
    for block in range(BLK_DEV):
        scores = jnp.where(block_in == block, every[:, block * BLK : (block + 1) * BLK], scores)
    row_top = jnp.max(jnp.where(valid_in, scores, -1e30), axis=1, keepdims=True)
    expo = jnp.where(valid_in, jnp.exp(scores - row_top), 0.0)
    row_total = jnp.maximum(jnp.sum(expo, axis=1, keepdims=True), 1e-30)
    row_lse = row_top + jnp.log(row_total)
    mean_item = nn(spread(expo / row_total), items)
    mean_in = exchange(mean_item)
    lse_in = exchange(row_lse)
    mine = member_row > 0.5
    query_max = jnp.max(jnp.where(mine, lse_in, -jnp.inf), axis=0, keepdims=True)
    row_max = jnp.sum(jnp.where(mine, query_max, 0.0), axis=1, keepdims=True)
    used_row = jnp.sum(member_row, axis=1, keepdims=True) > 0.5
    weight = jnp.where(used_row, jnp.exp(lse_in - row_max), 0.0)
    query_sum = jnp.sum(jnp.where(mine, weight, 0.0), axis=0, keepdims=True)
    scale = n_cand[None, :] / query_sum
    row_weight = jnp.where(mine, weight * scale, 0.0)
    query_gradient = tn(row_weight, mean_in, HI) - query_teacher
    shift = query_max - jnp.log(scale)
    row_shift = jnp.sum(jnp.where(mine, shift, 0.0), axis=1, keepdims=True)
    shift_in = exchange(row_shift)
    dlogit = jnp.where(valid_in, jnp.exp(scores - shift_in), 0.0) - teacher_in
    grad_items = tn(spread(dlogit), query_in)
    grad_emb = (
        inv_rms
        * (
            query_gradient
            - emb_raw
            * inv_rms
            * inv_rms
            * jnp.mean(query_gradient * emb_raw, axis=1, keepdims=True)
        )
    ).astype(BF16)
    grad_emb_all = lax.all_gather(grad_emb, "sub", axis=0, tiled=True)
    embed_term = tn(hidden, grad_emb_all)
    dhidden = nt(grad_emb_all, w_embed)
    sig = jax.nn.sigmoid(preact)
    grad_pre = (dhidden * sig * (1.0 + preact * (1.0 - sig))).astype(BF16)
    grad_feats = lax.psum_scatter(
        nt(grad_pre, w_hidden).astype(BF16), "sub", scatter_dimension=0, tiled=True
    ).astype(F32)
    hidden_term = tn(gathered, grad_pre).astype(BF16)
    width = hidden_term.shape[1]
    joined = jnp.concatenate(
        [
            hidden_term.reshape(n_shard, -1, width),
            embed_term.astype(BF16).reshape(n_shard, -1, width),
        ],
        axis=1,
    )
    joined = lax.psum_scatter(joined, "shard", scatter_dimension=0, tiled=False)
    depth = hidden_term.shape[0] // n_shard
    grad_hidden = joined[:depth].astype(F32)
    embed_part = joined[depth:].reshape(-1, embed_term.shape[1])
    grad_embed = lax.all_gather(embed_part, "shard", axis=0, tiled=True).astype(F32)
    return (grad_feats, grad_hidden, grad_embed, grad_items)


def solution(mesh):
    both = ("shard", "sub")
    placed = (
        P(both, None),
        P(None, "sub"),
        P("sub", None),
        P(both, None),
        P(both, None),
        P(both, None),
        P(both),
        P(both, None),
        P(both),
    )
    return jax.shard_map(
        per_device,
        mesh=mesh,
        in_specs=placed,
        out_specs=(P(both, None), P("shard", "sub"), P("sub", None), P(both, None)),
        check_vma=False,
    )
```

time: 786 us -> 588 us (0.75)
  other arithmetic: 147 us -> 31.5 us
  waiting for transfers between devices: 412 us -> 337 us
  starting transfers between devices: 41.6 us -> 77.6 us
  blocking collectives: 77.3 us -> 60 us
  local copies, waits for them, and re-layouts: 51.6 us -> 36 us
    psum x1 -> x0, waiting for transfers between devices: 142 us -> none  [per_device(): grad_embed = lax.psum(embed_term_local, 'shard')]
    gather x8 -> x0, other arithmetic: 120 us -> none  [the longest x2 39.9 us: query_softmax(): return expo / query_count_total[local_query][:, None]]
    all_to_all x6 -> x14, waiting for transfers between devices: 14.7 us -> 106 us  [the longest x7 73.4 us: exchange(): lax.all_to_all(array, 'shard', split_axis=0, concat_axis=0, tiled=True)]
    all_to_all x4 -> x0, blocking collectives: 68.2 us -> none  [the longest x1 23.3 us: per_device(): lax.all_to_all(dlogit_buf, 'shard', split_axis=0, concat_axis=0, tiled=True)]
    all_gather x0 -> x1, blocking collectives: none -> 50.8 us  [per_device(): lax.all_gather(embed_part, 'shard', axis=0, tiled=True).astype(F32)]
    all_to_all x6 -> x14, starting transfers between devices: 41.2 us -> 77.5 us  [the longest x7 53.9 us: exchange(): lax.all_to_all(array, 'shard', split_axis=0, concat_axis=0, tiled=True)]
    reduce_scatter x2, waiting for transfers between devices: 51.9 us -> 17.6 us  [the longest x1 17.6 us: per_device(): lax.psum_scatter(nn(hidden, w_embed), 'sub', scatter_dimension=0, tiled=T...]
    not x1 -> x0, other arithmetic: 19.8 us -> none  [per_device(): jnp.logical_not(is_last)[:, None]]
  transfers between devices with their start and end apart: 11 -> 18, of which waited for: 7 -> 15; matrix products, arithmetic and copies ran while one was open for 16% -> 11% of each run, Pallas kernels for 0% -> 0%
where the time goes in v1:
time: 588 us; the launch traced here: 586 us
  waiting for transfers between devices  337 us (57%)
  starting transfers between devices  77.6 us (13%)
  blocking collectives  60 us (10%)
  local copies, waits for them, and re-layouts  36 us (6%)
  other arithmetic  31.5 us (5%)
  matrix products  30.4 us (5%)
  between operations  14.3 us (2%)
    unnamed x5, waiting for transfers between devices  201 us
    all_to_all x7, waiting for transfers between devices, exchange(): lax.all_to_all(array, 'shard', split_axis=0, concat_axis=0, tiled=True)  73.4 us
    all_to_all x7, starting transfers between devices, exchange(): lax.all_to_all(array, 'shard', split_axis=0, concat_axis=0, tiled=True)  53.9 us
    all_gather x1, blocking collectives, per_device(): lax.all_gather(embed_part, 'shard', axis=0, tiled=True).astype(F32)  50.8 us
    all_to_all x7, waiting for transfers between devices, exchange(): lax.all_to_all(array, 'sub', split_axis=1, concat_axis=1, tiled=True)  32.5 us
    dot_general x15, matrix products, dot(): lax.dot_general(left, right, ((dims[0], dims[1]), ((), ())), precision=pr...  30.4 us
    all_to_all x7, starting transfers between devices, exchange(): lax.all_to_all(array, 'sub', split_axis=1, concat_axis=1, tiled=True)  23.6 us
    reduce_scatter x1, waiting for transfers between devices, per_device(): lax.psum_scatter(nn(hidden, w_embed), 'sub', scatter_dimension=0, tiled=T...  17.6 us
  transfers between devices with their start and end apart: 18, of which 15 were waited for; matrix products, arithmetic and copies ran while one was open for 11% of the time, Pallas kernels for 0%

profile of v1, /device:TPU:1, one launch (start us, length us, event | category | flops | bytes accessed | tf_op | source)
XLA Modules:
  0.0 586.4 jit_solution(8655140551144212763)
XLA Ops:
  14.0 13.0 %all-to-all-start = ((s32[64,4,2]{1,2,0:T(2,128)}), s32[64,4,2]{1,2,0:T(2,128)S(1)}, u32[]{:S(2)}, u32[]{:S(2)}) async-start(s32[64,4,2]{1,2,0:T(2,128)} %copy.85), calls=%async_computation.1 | async-start | bytes 131072 | tf_op jit(solution)/shard_map/all_to_all | solution.py:37
  27.1 12.2 %all-gather.2.cloned.1.call-done = bf16[128,4096]{1,0:T(8,128)(2,1)} async-done(((bf16[32,4096]{1,0:T(8,128)(2,1)}), bf16[128,4096]{1,0:T(8,128)(2,1)}) %all-gather.2.cloned.1.call-update) | async-done | bytes 1048592 | tf_op jit(solution)/shard_map/all_gather | solution.py:86
  39.3 5.8 multiply_convert_fusion
  50.6 17.6 %reduce-scatter.3.cloned.1.call-done = f32[32,256]{1,0:T(8,128)} async-done(((f32[128,256]{1,0:T(8,128)}), f32[32,256]{1,0:T(8,128)}) %reduce-scatter.3.cloned.1.call-update) | async-done | bytes 32784 | tf_op jit(solution)/shard_map/reduce_scatter | solution.py:89
  70.9 12.8 %all-to-all-start.2 = ((bf16[64,4,2,256]{3,2,1,0:T(2,128)(2,1)}), bf16[64,4,2,256]{3,2,1,0:T(2,128)(2,1)S(1)}, u32[]{:S(2)}, u32[]{:S(2)}) async-start(bf16[64,4,2,256]{3,2,1,0:T(2,128)(2,1)} %reshape.514), calls=%async_computation.3 | async-start | bytes 524288 | tf_op jit(solution)/shard_map/all_to_all | solution.py:37
  85.4 11.5 %all-to-all-done.2 = bf16[64,4,2,256]{3,2,1,0:T(2,128)(2,1)S(1)} async-done(((bf16[64,4,2,256]{3,2,1,0:T(2,128)(2,1)}), bf16[64,4,2,256]{3,2,1,0:T(2,128)(2,1)S(1)}, u32[]{:S(2)}, u32[]{:S(2)}) %all-to-all-start.2) | async-done | bytes 262176 | tf_op jit(solution)/shard_map/all_to_all | solution.py:37
  101.2 6.5 %all-to-all-done.3 = bf16[64,4,2,256]{3,2,0,1:T(2,128)(2,1)S(1)} async-done(((bf16[64,4,2,256]{3,2,0,1:T(2,128)(2,1)}), bf16[64,4,2,256]{3,2,0,1:T(2,128)(2,1)S(1)}, u32[]{:S(2)}, u32[]{:S(2)}) %all-to-all-start.3) | async-done | bytes 262176 | tf_op jit(solution)/shard_map/all_to_all | solution.py:38
  116.9 9.9 %all-to-all-done.4 = f32[64,4,2,1]{1,2,3,0:T(2,128)S(1)} async-done(((f32[64,4,2,1]{1,2,3,0:T(2,128)}), f32[64,4,2,1]{1,2,3,0:T(2,128)S(1)}, u32[]{:S(2)}, u32[]{:S(2)}) %all-to-all-start.4) | async-done | bytes 2080 | tf_op jit(solution)/shard_map/all_to_all | solution.py:37
  138.2 5.6 all-to-all-start.12
  145.1 8.8 %all-to-all-done.12 = f32[64,4,2,1]{1,2,3,0:T(2,128)S(1)} async-done(((f32[64,4,2,1]{1,2,3,0:T(2,128)}), f32[64,4,2,1]{1,2,3,0:T(2,128)S(1)}, u32[]{:S(2)}, u32[]{:S(2)}) %all-to-all-start.12) | async-done | bytes 2080 | tf_op jit(solution)/shard_map/all_to_all | solution.py:37
  159.2 12.5 %all-to-all-done.8 = f32[64,4,2,128]{3,2,1,0:T(2,128)S(1)} async-done(((f32[64,4,2,128]{3,2,1,0:T(2,128)}), f32[64,4,2,128]{3,2,1,0:T(2,128)S(1)}, u32[]{:S(2)}, u32[]{:S(2)}) %all-to-all-start.8) | async-done | bytes 262176 | tf_op jit(solution)/shard_map/all_to_all | solution.py:37
  197.9 7.0 %all-to-all-start.6 = ((f32[64,4,2,256]{3,2,1,0:T(2,128)}), f32[64,4,2,256]{3,2,1,0:T(2,128)S(1)}, u32[]{:S(2)}, u32[]{:S(2)}) async-start(f32[64,4,2,256]{3,2,1,0:T(2,128)} %copy.95), calls=%async_computation.7 | async-start | bytes 1048576 | tf_op jit(solution)/shard_map/all_to_all | solution.py:37
  208.7 14.0 %all-to-all-done.6 = f32[64,4,2,256]{3,2,1,0:T(2,128)S(1)} async-done(((f32[64,4,2,256]{3,2,1,0:T(2,128)}), f32[64,4,2,256]{3,2,1,0:T(2,128)S(1)}, u32[]{:S(2)}, u32[]{:S(2)}) %all-to-all-start.6) | async-done | bytes 524320 | tf_op jit(solution)/shard_map/all_to_all | solution.py:37
  222.7 5.7 all-to-all-start.10
  229.4 16.7 %all-to-all-done.10 = f32[64,4,2,256]{3,2,1,0:T(2,128)S(1)} async-done(((f32[64,4,2,256]{3,2,1,0:T(2,128)}), f32[64,4,2,256]{3,2,1,0:T(2,128)S(1)}, u32[]{:S(2)}, u32[]{:S(2)}) %all-to-all-start.10) | async-done | bytes 524320 | tf_op jit(solution)/shard_map/all_to_all | solution.py:37
  250.6 8.2 %all-to-all-done.7 = f32[64,4,2,256]{3,2,0,1:T(2,128)S(1)} async-done(((f32[64,4,2,256]{3,2,0,1:T(2,128)}), f32[64,4,2,256]{3,2,0,1:T(2,128)S(1)}, u32[]{:S(2)}, u32[]{:S(2)}) %all-to-all-start.7) | async-done | bytes 524320 | tf_op jit(solution)/shard_map/all_to_all | solution.py:38
  262.9 7.3 %all-to-all-done.11 = f32[64,4,2,256]{3,2,0,1:T(2,128)S(1)} async-done(((f32[64,4,2,256]{3,2,0,1:T(2,128)}), f32[64,4,2,256]{3,2,0,1:T(2,128)S(1)}, u32[]{:S(2)}, u32[]{:S(2)}) %all-to-all-start.11) | async-done | bytes 524320 | tf_op jit(solution)/shard_map/all_to_all | solution.py:38
  271.8 9.2 %all_gather.10 = bf16[128,256]{1,0:T(8,128)(2,1)S(1)} all-gather(bf16[32,256]{1,0:T(8,128)(2,1)S(1)} %multiply_convert_fusion.1), channel_id=1, replica_groups=mesh['shard'=64,'sub'=4] {'sub'}, dimensions={0}, use_global_device_ids=true | all-gather | bytes 81920 | tf_op jit(solution)/shard_map/all_gather | solution.py:128
  282.6 7.2 %convolution_convert_fusion = bf16[128,4096]{1,0:T(8,128)(2,1)} fusion(bf16[128,1024]{1,0:T(8,128)(2,1)S(1)} %fusion.3, bf16[4096,1024]{1,0:T(8,128)(2,1)} %param.10), kind=kOutput, calls=%fused_computation.2 | convolution fusion | flops 1074266112 | bytes 9699328 | tf_op jit(solution)/shard_map/dot_general | solution.py:16
  289.9 5.6 convert_bitcast_fusion
  295.5 12.0 %copy.104 = bf16[4096,1024]{1,0:T(8,128)(2,1)} copy(bf16[4096,1024]{0,1:T(8,128)(2,1)} %convert_bitcast_fusion) | data formatting | bytes 16777216 | tf_op jit(solution)/shard_map/convert_element_type | solution.py:136
  308.0 8.8 %pad_maximum_fusion = bf16[64,68,1024]{2,1,0:T(8,128)(2,1)} fusion(bf16[64,4,1024]{2,1,0:T(4,128)(2,1)S(1)} %reshape.521, bf16[64,64,1024]{2,1,0:T(8,128)(2,1)} %bitcast.68), kind=kLoop, calls=%fused_computation | loop fusion | flops 17825792 | bytes 17825792 | tf_op jit(solution)/shard_map/concatenate | solution.py:138
  324.2 200.2 %all-reduce.3.cloned.1.call-done = bf16[64,68,1024]{2,1,0:T(8,128)(2,1)} async-done(((bf16[64,68,1024]{2,1,0:T(8,128)(2,1)}), bf16[64,68,1024]{2,1,0:T(8,128)(2,1)}) %all-reduce.3.cloned.1.call-update) | async-done | bytes 8912912
  525.7 50.8 %all_gather.11 = bf16[1024,256]{1,0:T(8,128)(2,1)S(1)} all-gather(bf16[16,256]{1,0:T(8,128)(2,1)S(1)} %reshape.522), channel_id=1, replica_groups=mesh['shard'=64,'sub'=4] {'shard'}, dimensions={0}, use_global_device_ids=true | all-gather | bytes 532480 | tf_op jit(solution)/shard_map/all_gather | solution.py:149
  (145 shorter events, 103.2 us)
Async XLA Ops:
  7.2 100.8 %copy-start = (bf16[1024,256]{1,0:T(8,128)(2,1)S(1)}, bf16[1024,256]{1,0:T(8,128)(2,1)}, u32[]{:S(2)}) copy-start(bf16[1024,256]{1,0:T(8,128)(2,1)} %param.12) | copy-start | bytes 1572868
  7.2 32.1 %all-gather.2.cloned.1.call-start = ((), (), s32[]{:S(2)}) async-start(), calls=%async_computation.16 | async-start | bytes 1310720 | tf_op jit(solution)/shard_map/all_gather | solution.py:86
  14.0 32.6 %all-to-all-start = ((s32[64,4,2]{1,2,0:T(2,128)}), s32[64,4,2]{1,2,0:T(2,128)S(1)}, u32[]{:S(2)}, u32[]{:S(2)}) async-start(s32[64,4,2]{1,2,0:T(2,128)} %copy.85), calls=%async_computation.1 | async-start | bytes 131072 | tf_op jit(solution)/shard_map/all_to_all | solution.py:37
  27.0 41.1 %reduce-scatter.3.cloned.1.call-start = ((), (), s32[]{:S(2)}) async-start(), calls=%async_computation.17 | async-start | bytes 163840 | tf_op jit(solution)/shard_map/reduce_scatter | solution.py:89
  45.1 91.7 %copy-start.7 = (s32[1,32]{1,0:T(1,128)S(1)}, s32[1,32]{1,0:T(1,128)}, u32[]{:S(2)}) copy-start(s32[1,32]{1,0:T(1,128)} %param.14) | copy-start | bytes 388
  45.1 91.7 %copy-start.8 = (s32[32]{0:T(128)S(1)}, s32[32]{0:T(128)}, u32[]{:S(2)}) copy-start(s32[32]{0:T(128)} %param.15) | copy-start | bytes 388
  47.4 23.5 %all-to-all-start.1 = ((s32[4,1,128]{2,1,0:T(1,128)}), s32[4,1,128]{2,1,0:T(1,128)S(1)}, u32[]{:S(2)}, u32[]{:S(2)}) async-start(s32[4,1,128]{2,1,0:T(1,128)} %reshape.528), calls=%async_computation.2 | async-start | bytes 4096 | tf_op jit(solution)/shard_map/all_to_all | solution.py:38
  70.9 26.0 %all-to-all-start.2 = ((bf16[64,4,2,256]{3,2,1,0:T(2,128)(2,1)}), bf16[64,4,2,256]{3,2,1,0:T(2,128)(2,1)S(1)}, u32[]{:S(2)}, u32[]{:S(2)}) async-start(bf16[64,4,2,256]{3,2,1,0:T(2,128)(2,1)} %reshape.514), calls=%async_computation.3 | async-start | bytes 524288 | tf_op jit(solution)/shard_map/all_to_all | solution.py:37
  97.8 9.9 %all-to-all-start.3 = ((bf16[64,4,2,256]{3,2,0,1:T(2,128)(2,1)}), bf16[64,4,2,256]{3,2,0,1:T(2,128)(2,1)S(1)}, u32[]{:S(2)}, u32[]{:S(2)}) async-start(bf16[64,4,2,256]{3,2,0,1:T(2,128)(2,1)} %copy.88), calls=%async_computation.4 | async-start | bytes 524288 | tf_op jit(solution)/shard_map/all_to_all | solution.py:38
  111.4 15.3 %all-to-all-start.4 = ((f32[64,4,2,1]{1,2,3,0:T(2,128)}), f32[64,4,2,1]{1,2,3,0:T(2,128)S(1)}, u32[]{:S(2)}, u32[]{:S(2)}) async-start(f32[64,4,2,1]{1,2,3,0:T(2,128)} %copy.90), calls=%async_computation.5 | async-start | bytes 131072 | tf_op jit(solution)/shard_map/all_to_all | solution.py:37
  127.5 7.2 %all-to-all-start.5 = ((f32[4,1,128]{2,1,0:T(1,128)}), f32[4,1,128]{2,1,0:T(1,128)S(1)}, u32[]{:S(2)}, u32[]{:S(2)}) async-start(f32[4,1,128]{2,1,0:T(1,128)} %reshape.530), calls=%async_computation.6 | async-start | bytes 4096 | tf_op jit(solution)/shard_map/all_to_all | solution.py:38
  138.2 15.7 %all-to-all-start.12 = ((f32[64,4,2,1]{1,2,3,0:T(2,128)}), f32[64,4,2,1]{1,2,3,0:T(2,128)S(1)}, u32[]{:S(2)}, u32[]{:S(2)}) async-start(f32[64,4,2,1]{1,2,3,0:T(2,128)} %copy.105), calls=%async_computation.14 | async-start | bytes 131072 | tf_op jit(solution)/shard_map/all_to_all | solution.py:37
  153.9 17.7 %all-to-all-start.8 = ((f32[64,4,2,128]{3,2,1,0:T(2,128)}), f32[64,4,2,128]{3,2,1,0:T(2,128)S(1)}, u32[]{:S(2)}, u32[]{:S(2)}) async-start(f32[64,4,2,128]{3,2,1,0:T(2,128)} %bitcast.6), calls=%async_computation.9 | async-start | bytes 524288 | tf_op jit(solution)/shard_map/all_to_all | solution.py:37
  171.6 7.2 %all-to-all-start.13 = ((f32[4,1,128]{2,1,0:T(1,128)}), f32[4,1,128]{2,1,0:T(1,128)S(1)}, u32[]{:S(2)}, u32[]{:S(2)}) async-start(f32[4,1,128]{2,1,0:T(1,128)} %reshape.532), calls=%async_computation.15 | async-start | bytes 4096 | tf_op jit(solution)/shard_map/all_to_all | solution.py:38
  178.9 8.9 %all-to-all-start.9 = ((f32[64,4,2,128]{3,2,0,1:T(2,128)}), f32[64,4,2,128]{3,2,0,1:T(2,128)S(1)}, u32[]{:S(2)}, u32[]{:S(2)}) async-start(f32[64,4,2,128]{3,2,0,1:T(2,128)} %copy.98), calls=%async_computation.10 | async-start | bytes 524288 | tf_op jit(solution)/shard_map/all_to_all | solution.py:38
  195.5 75.7 %copy-start.5 = (f32[32,256]{1,0:T(8,128)S(1)}, f32[32,256]{1,0:T(8,128)}, u32[]{:S(2)}) copy-start(f32[32,256]{1,0:T(8,128)} %reduce-scatter.3.cloned.1.call-done) | copy-start | bytes 98308
  197.9 24.8 %all-to-all-start.6 = ((f32[64,4,2,256]{3,2,1,0:T(2,128)}), f32[64,4,2,256]{3,2,1,0:T(2,128)S(1)}, u32[]{:S(2)}, u32[]{:S(2)}) async-start(f32[64,4,2,256]{3,2,1,0:T(2,128)} %copy.95), calls=%async_computation.7 | async-start | bytes 1048576 | tf_op jit(solution)/shard_map/all_to_all | solution.py:37
  222.7 23.4 %all-to-all-start.10 = ((f32[64,4,2,256]{3,2,1,0:T(2,128)}), f32[64,4,2,256]{3,2,1,0:T(2,128)S(1)}, u32[]{:S(2)}, u32[]{:S(2)}) async-start(f32[64,4,2,256]{3,2,1,0:T(2,128)} %copy.101), calls=%async_computation.11 | async-start | bytes 1048576 | tf_op jit(solution)/shard_map/all_to_all | solution.py:37
  246.1 12.6 %all-to-all-start.7 = ((f32[64,4,2,256]{3,2,0,1:T(2,128)}), f32[64,4,2,256]{3,2,0,1:T(2,128)S(1)}, u32[]{:S(2)}, u32[]{:S(2)}) async-start(f32[64,4,2,256]{3,2,0,1:T(2,128)} %copy.96), calls=%async_computation.8 | async-start | bytes 1048576 | tf_op jit(solution)/shard_map/all_to_all | solution.py:38
  258.8 11.4 %all-to-all-start.11 = ((f32[64,4,2,256]{3,2,0,1:T(2,128)}), f32[64,4,2,256]{3,2,0,1:T(2,128)S(1)}, u32[]{:S(2)}, u32[]{:S(2)}) async-start(f32[64,4,2,256]{3,2,0,1:T(2,128)} %copy.102), calls=%async_computation.12 | async-start | bytes 1048576 | tf_op jit(solution)/shard_map/all_to_all | solution.py:38
  262.3 60.1 %reduce-scatter.5.cloned.1.call-start = ((), (), s32[]{:S(2)}) async-start(), calls=%async_computation.18 | async-start | bytes 1310720 | tf_op jit(solution)/shard_map/reduce_scatter | solution.py:133
  270.4 19.5 %copy-start.2 = (bf16[128,4096]{1,0:T(8,128)(2,1)S(1)}, bf16[128,4096]{1,0:T(8,128)(2,1)}, u32[]{:S(2)}) copy-start(bf16[128,4096]{1,0:T(8,128)(2,1)} %all-gather.2.cloned.1.call-done) | copy-start | bytes 3145732
  289.8 234.5 %all-reduce.3.cloned.1.call-start = ((), (), s32[]{:S(2)}) async-start(), calls=%async_computation.19 | async-start | bytes 18874368
  308.0 271.8 %copy-start.1 = (bf16[1024,256]{1,0:T(8,128)(2,1)S(1)}, bf16[1024,256]{1,0:T(8,128)(2,1)}, u32[]{:S(2)}) copy-start(bf16[1024,256]{1,0:T(8,128)(2,1)} %param.12) | copy-start | bytes 1572868
  (4 other events, 39.2 us)
Sparse Core Ops, SparseCore 0:
  9.8 29.4 all-gather.1
  46.1 21.9 reduce-scatter.2
  290.0 24.1 reduce-scatter.4
  317.6 206.7 all-reduce.2

commit v2 on v1

v2 whole, which is shorter than its diff:
```python
import functools

import jax
import jax.numpy as jnp
from jax import lax
from jax.experimental import pallas as pl
from jax.experimental.pallas import tpu as pltpu
from jax.sharding import PartitionSpec as P

BLK = 128
BLK_DEV = 8
CAP = 2
EPS = 1e-06
F32 = jnp.float32
BF16 = jnp.bfloat16
I32 = jnp.int32
MESH = pl.DeviceIdType.MESH
STAGES = (
    "feats", "emb", "e1a", "e1b", "e2b", "e2a", "e3a", "e3b", "e4b", "e4a", "e5a", "e5b",
    "px", "fx", "gy", "gx", "core", "zs", "gf0", "gf1", "gf2", "gf3", "er", "eb", "ex",
)


def dot(left, right, left_dim, right_dim):
    return lax.dot_general(
        left, right, (((left_dim,), (right_dim,)), ((), ())), preferred_element_type=F32
    )


def nn(left, right):
    return dot(left, right, 1, 0)


def tn(left, right):
    return dot(left, right, 0, 0)


def nt(left, right):
    return dot(left, right, 1, 1)


def iota(shape, axis):
    return lax.broadcasted_iota(I32, shape, axis)


def pieces(value):
    high = value.astype(BF16).astype(F32)
    rest = value - high
    middle = rest.astype(BF16).astype(F32)
    return high, middle, rest - middle


def in_lanes(columns, rows):
    lane = iota((rows, 128), 1)
    result = jnp.zeros((rows, 128), F32)
    for place, column in enumerate(columns):
        result = jnp.where(lane == place, column, result)
    return result


def kernel(n_z, n_x, n_y, names, *refs):
    r = dict(zip(names, refs))
    feats, w_hbm, w_embed, items = r["feats"], r["w_hidden"], r["w_embed"], r["items"]
    n_a, n_b = n_x * n_y, n_z * 2
    rows = n_a * n_b * CAP
    q_dev, depth = feats.shape
    units = w_hbm.shape[1]
    emb = w_embed.shape[1]
    slots = r["teacher"].shape[0]
    block_cols = depth // (n_z * n_x)
    half = block_cols // 2

    shard, y = lax.axis_index("shard"), lax.axis_index("sub")
    core = lax.rem(shard, 2)
    x = lax.rem(shard // 2, n_x)
    z = shard // (2 * n_x)
    a = x * n_y + y
    b = z * 2 + core

    def at(z_, x_, core_, y_):
        return ((z_ * n_x + x_) * 2 + core_, y_)

    groups = {
        "y": (n_y, y, lambda p: at(z, x, core, p)),
        "x": (n_x, x, lambda p: at(z, p, core, y)),
        "z": (n_z, z, lambda p: at(p, x, core, y)),
        "a": (n_a, a, lambda p: at(z, p // n_y, core, lax.rem(p, n_y))),
        "b": (n_b, b, lambda p: at(p // 2, x, lax.rem(p, 2), y)),
    }
    send_sem, recv_sem = r["send_sem"], r["recv_sem"]
    pending = []

    def remote(stage, source, target, send_at, recv_at, device):
        row = STAGES.index(stage)
        return pltpu.make_async_remote_copy(
            src_ref=source,
            dst_ref=target,
            send_sem=send_sem.at[row, send_at],
            recv_sem=recv_sem.at[row, recv_at],
            device_id=device,
            device_id_type=MESH,
        )

    def each(group, body):
        size, me, device = groups[group]

        def step(j, carry):
            body(lax.rem(me + j, size), me, device)
            return carry

        lax.fori_loop(1, size, step, 0)

    def send(stage, group, source, target):
        def start(p, me, device):
            remote(stage, source(p), target(me), p, me, device(p)).start()

        each(group, start)

        def finish():
            def wait(p, me, device):
                remote(stage, source(p), target(me), p, me, device(p)).wait_send()

            each(group, wait)

        pending.append(finish)

    def receive(stage, group, target):
        def wait(p, me, device):
            remote(stage, target(p), target(p), p, p, device(p)).wait_recv()

        each(group, wait)

    weights = r["weights"]
    load = pltpu.make_async_copy(w_hbm, weights, r["load_sem"])
    load.start()
    barrier = pltpu.get_barrier_semaphore()
    for group in ("a", "b"):
        each(
            group,
            lambda p, me, device: pl.semaphore_signal(
                barrier, inc=1, device_id=device(p), device_id_type=MESH
            ),
        )
    feats_y = r["feats_y"]
    feats_y[y] = feats[...]
    pl.semaphore_wait(barrier, n_a + n_b - 2)
    send("feats", "y", lambda p: feats, lambda me: feats_y.at[me])

    perm = r["perm"]
    log_a, log_b = n_a.bit_length() - 1, n_b.bit_length() - 1
    line = iota((rows, rows), 0)
    from_row = (
        jnp.bitwise_and(line >> 1, n_a - 1) * (2 * n_b)
        + (line >> (1 + log_a)) * 2
        + jnp.bitwise_and(line, 1)
    )
    perm[...] = jnp.where(from_row == iota((rows, rows), 1), 1.0, 0.0).astype(BF16)

    def first(name, forward):
        group, size = ("a", n_a) if forward else ("b", n_b)
        source, target = r[name + "_s1"], r[name + "_r1"]
        me = groups[group][1]
        send(name + group, group, lambda p: source.at[p], lambda m: target.at[m])
        target[me] = source[me]

    def second(name, forward):
        group, size = ("a", n_a) if forward else ("b", n_b)
        other, other_size = ("b", n_b) if forward else ("a", n_a)
        middle = r[name + "_r1"]
        receive(name + group, group, lambda p: middle.at[p])
        source, target = r[name + "_s2"], r[name + "_r2"]
        lanes = middle.shape[2]
        moved = nn(perm[...], middle[...].reshape(rows, lanes)).astype(BF16)
        source[...] = moved.reshape(other_size, rows // other_size, lanes)
        me = groups[other][1]
        send(name + other, other, lambda p: source.at[p], lambda m: target.at[m])
        target[me] = source[me]

    def third(name, forward):
        other = "b" if forward else "a"
        target = r[name + "_r2"]
        receive(name + other, other, lambda p: target.at[p])
        return target

    counts = r["counts"][...].astype(F32)
    tails = r["tails"][...].astype(F32)
    triangle = jnp.where(iota((q_dev, q_dev), 0) <= iota((q_dev, q_dev), 1), 1.0, 0.0)
    ends = nn(jnp.broadcast_to(counts, (8, q_dev)).astype(BF16), triangle.astype(BF16))[0:1]
    starts = ends - counts
    pos = iota((slots, q_dev), 0).astype(F32)
    member = jnp.logical_and(pos < ends, pos >= starts)
    used = jnp.where(pos == ends - 1.0, tails, float(BLK))
    slot_used = jnp.sum(jnp.where(member, used, 0.0), axis=1, keepdims=True)
    valid = iota((slots, BLK), 1).astype(F32) < slot_used
    n_cand = (counts - 1.0) * BLK + tails
    logit = r["teacher"][...].astype(F32)
    top = jnp.max(jnp.where(valid, logit, -1e30), axis=1, keepdims=True)
    query_top = jnp.max(jnp.where(member, top, -1e30), axis=0, keepdims=True)
    slot_top = jnp.sum(jnp.where(member, query_top, 0.0), axis=1, keepdims=True)
    expo = jnp.where(valid, jnp.exp(logit - slot_top), 0.0)
    slot_sum = jnp.sum(expo, axis=1, keepdims=True)
    total = jnp.sum(jnp.where(member, slot_sum, 0.0), axis=0, keepdims=True)
    query_shift = query_top + jnp.log(total / n_cand)
    slot_shift = jnp.sum(jnp.where(member, query_shift, 0.0), axis=1, keepdims=True)
    owner = r["owner"][...]
    same = jnp.logical_and(
        r["owner_row"][...] == owner, iota((slots, slots), 1) < iota((slots, slots), 0)
    )
    rank = jnp.sum(jnp.where(same, 1.0, 0.0), axis=1, keepdims=True)
    log_y, log_x = n_y.bit_length() - 1, n_x.bit_length() - 1
    owner_y = jnp.bitwise_and(owner, n_y - 1)
    owner_core = jnp.bitwise_and(owner >> log_y, 1)
    owner_x = jnp.bitwise_and(owner >> (log_y + 1), n_x - 1)
    owner_z = owner >> (log_y + 1 + log_x)
    base = ((owner_x * n_y + owner_y) * n_b + owner_z * 2 + owner_core) * CAP
    dest = base.astype(F32) + rank
    place = jnp.where(dest == iota((slots, rows), 1).astype(F32), 1.0, 0.0).astype(BF16)
    side = in_lanes((r["block"][...].astype(F32), slot_used) + pieces(slot_shift), slots)
    payload = jnp.concatenate([logit, side], axis=1).astype(BF16)
    r["e1_s1"][...] = tn(place, payload).astype(BF16).reshape(r["e1_s1"].shape)
    first("e1", True)
    member_row = r["member_row"]
    member_row[...] = tn(place, jnp.where(member, 1.0, 0.0).astype(BF16))
    second("e1", True)

    receive("feats", "y", lambda p: feats_y.at[p])
    load.wait()
    preact, preact_x = r["preact"], r["preact_x"]
    group_rows = n_y * q_dev
    everyone = feats_y[...].reshape(group_rows, depth)
    step_units = min(256, units)

    def forward(j, total_emb):
        columns = pl.ds(pl.multiple_of(j * step_units, step_units), step_units)
        part = nn(everyone, weights[:, columns])
        preact[:, columns] = part
        hidden = (part / (1.0 + jnp.exp(-part))).astype(BF16)
        return total_emb + nn(hidden, w_embed[columns, :])

    emb_part = lax.fori_loop(
        0, units // step_units, forward, jnp.zeros((group_rows, emb), F32)
    )
    emb_s, emb_r = r["emb_s"], r["emb_r"]
    emb_s[...] = emb_part.reshape(n_y, q_dev, emb)
    send("emb", "y", lambda p: emb_s.at[p], lambda me: emb_r.at[me])
    emb_r[y] = emb_s[y]

    chunks = max(1, rows // 128)
    per = n_b // chunks
    chunk_rows = rows // chunks

    def lift(values, block_in):
        parts = [jnp.where(block_in == float(k), values, 0.0).astype(BF16) for k in range(BLK_DEV)]
        return jnp.concatenate(parts, axis=1)

    sent = third("e1", True)
    teacher_n, info, spread = r["teacher_n"], r["info"], r["spread"]

    def chunk_of(ref, j):
        return ref[pl.ds(j * per, per)].reshape(chunk_rows, ref.shape[2])

    def rows_of(j):
        return pl.ds(pl.multiple_of(j * chunk_rows, chunk_rows), chunk_rows)

    def teacher_part(j, carry):
        chunk = chunk_of(sent, j).astype(F32)
        notes = chunk[:, BLK : 2 * BLK]
        block_in, used_in = notes[:, 0:1], notes[:, 1:2]
        shift_in = notes[:, 2:3] + notes[:, 3:4] + notes[:, 4:5]
        valid_in = iota((chunk_rows, BLK), 1).astype(F32) < used_in
        probs = jnp.where(valid_in, jnp.exp(chunk[:, :BLK] - shift_in), 0.0)
        teacher_n[rows_of(j), :] = probs
        info[rows_of(j), :] = notes
        term = nn(lift(probs, block_in), items[...])
        r["e2_s1"][pl.ds(j * per, per)] = term.astype(BF16).reshape(per, 2 * n_a, emb)
        return carry

    lax.fori_loop(0, chunks, teacher_part, 0)
    first("e2", False)

    receive("emb", "y", lambda p: emb_r.at[p])
    emb_raw = jnp.sum(emb_r[...], axis=0)
    inv_rms = lax.rsqrt(jnp.mean(emb_raw * emb_raw, axis=1, keepdims=True) + EPS)
    query_emb = (emb_raw * inv_rms).astype(BF16)
    member_bf = member_row[...].astype(BF16)
    r["e3_s1"][...] = nn(member_bf, query_emb).astype(BF16).reshape(r["e3_s1"].shape)
    first("e3", True)
    second("e2", False)
    preact_x[x] = preact[...].astype(BF16)
    feats_s, feats_x = r["feats_s"], r["feats_x"]
    for p in range(n_x):
        for k in range(n_z):
            column = (k * n_x + p) * block_cols
            feats_s[p, :, k * block_cols : (k + 1) * block_cols] = feats_y[
                :, :, column : column + block_cols
            ].reshape(group_rows, block_cols)
    second("e3", True)
    send("px", "x", lambda p: preact_x.at[x], lambda me: preact_x.at[me])
    send("fx", "x", lambda p: feats_s.at[p], lambda me: feats_x.at[me])
    feats_x[x] = feats_s[x]
    back = third("e2", False)
    query_teacher = tn(member_bf, back[...].reshape(rows, emb))

    queries = third("e3", True)
    scores = r["scores"]

    def score_part(j, carry):
        every = nt(chunk_of(queries, j), items[...])
        notes = info[rows_of(j), :]
        block_in, used_in = notes[:, 0:1], notes[:, 1:2]
        picked = jnp.zeros((chunk_rows, BLK), F32)
        for k in range(BLK_DEV):
            picked = jnp.where(block_in == float(k), every[:, k * BLK : (k + 1) * BLK], picked)
        valid_in = iota((chunk_rows, BLK), 1).astype(F32) < used_in
        row_top = jnp.max(jnp.where(valid_in, picked, -1e30), axis=1, keepdims=True)
        row_expo = jnp.where(valid_in, jnp.exp(picked - row_top), 0.0)
        row_sum = jnp.maximum(jnp.sum(row_expo, axis=1, keepdims=True), 1e-30)
        scores[rows_of(j), :] = picked
        term = nn(lift(row_expo / row_sum, block_in), items[...])
        empty = used_in < 0.5
        lse = jnp.where(empty, 0.0, row_top + jnp.log(row_sum))
        message = jnp.concatenate([term, in_lanes(pieces(lse), chunk_rows)], axis=1)
        r["e4_s1"][pl.ds(j * per, per)] = message.astype(BF16).reshape(per, 2 * n_a, emb + 128)
        return carry

    lax.fori_loop(0, chunks, score_part, 0)
    first("e4", False)
    second("e4", False)
    returned = third("e4", False)[...].reshape(rows, emb + 128)

    lse_bits = returned[:, emb : emb + 128].astype(F32)
    lse_in = lse_bits[:, 0:1] + lse_bits[:, 1:2] + lse_bits[:, 2:3]
    mine = member_row[...] > 0.5
    query_max = jnp.max(jnp.where(mine, lse_in, -1e30), axis=0, keepdims=True)
    weight = jnp.where(mine, jnp.exp(lse_in - query_max), 0.0)
    scale = n_cand / jnp.sum(weight, axis=0, keepdims=True)
    weight = weight * scale
    weight_high = weight.astype(BF16)
    weight_low = (weight - weight_high.astype(F32)).astype(BF16)
    mean_item = returned[:, :emb]
    gradient = tn(weight_high, mean_item) + tn(weight_low, mean_item) - query_teacher
    grad_emb = (
        inv_rms
        * (
            gradient
            - emb_raw * inv_rms * inv_rms * jnp.mean(gradient * emb_raw, axis=1, keepdims=True)
        )
    ).astype(BF16)
    grad_y, grad_x = r["grad_y"], r["grad_x"]
    grad_y[y] = grad_emb
    send("gy", "y", lambda p: grad_y.at[y], lambda me: grad_y.at[me])
    shift = query_max - jnp.log(scale)
    row_shift = jnp.sum(jnp.where(mine, shift, 0.0), axis=1, keepdims=True)
    r["e5_s1"][...] = in_lanes(pieces(row_shift), rows).astype(BF16).reshape(r["e5_s1"].shape)
    first("e5", True)
    receive("gy", "y", lambda p: grad_y.at[p])
    grad_group = grad_y[...].reshape(group_rows, emb)
    grad_x[x] = grad_group
    send("gx", "x", lambda p: grad_x.at[x], lambda me: grad_x.at[me])

    def derivative(dhidden, before):
        sig = 1.0 / (1.0 + jnp.exp(-before))
        return (dhidden * sig * (1.0 + before * (1.0 - sig))).astype(BF16)

    grad_pre = derivative(nt(grad_group, w_embed[...]), preact[...])
    gf_s, gf_r = r["gf_s"], r["gf_r"]
    step_depth = min(256, depth // 4)

    def feats_part(part):
        quarter = depth // 4

        def step(j, carry):
            start = pl.multiple_of(part * quarter + j * step_depth, step_depth)
            value = nt(grad_pre, weights[pl.ds(start, step_depth), :])
            gf_s[:, :, pl.ds(start, step_depth)] = value.astype(BF16).reshape(
                n_y, q_dev, step_depth
            )
            return carry

        lax.fori_loop(0, quarter // step_depth, step, 0)
        columns = pl.ds(part * quarter, quarter)
        send(
            "gf" + str(part),
            "y",
            lambda p: gf_s.at[p, :, columns],
            lambda me: gf_r.at[me, :, columns],
        )

    feats_part(0)
    second("e5", True)
    receive("px", "x", lambda p: preact_x.at[p])
    receive("fx", "x", lambda p: feats_x.at[p])
    receive("gx", "x", lambda p: grad_x.at[p])

    pre_x = r["pre_x"]

    def pre_part(j, carry):
        pre_x[j] = derivative(nt(grad_x[j], w_embed[...]), preact_x[j].astype(F32))
        return carry

    lax.fori_loop(0, n_x, pre_part, 0)
    line_rows = n_x * group_rows
    halves, halves_bf, core_r = r["halves"], r["halves_bf"], r["core_r"]
    mate = at(z, x, 1 - core, y)

    def core_copy(k):
        return remote("core", halves_bf.at[k, 1 - core], core_r.at[k], k, k, mate)

    def hidden_part(j, carry):
        k = lax.rem(z + n_z // 2 + j, n_z)
        columns = pl.ds(pl.multiple_of(k * block_cols, block_cols), block_cols)
        left = feats_x[:, :, columns].reshape(line_rows, block_cols)
        value = tn(left, pre_x[...].reshape(line_rows, units)).reshape(2, half, units)
        halves[k] = value
        halves_bf[k] = value.astype(BF16)
        core_copy(k).start()
        return carry

    lax.fori_loop(0, n_z, hidden_part, 0)
    pending.append(
        lambda: lax.fori_loop(0, n_z, lambda k, s: (core_copy(k).wait_send(), s)[1], 0)
    )
    z_s, z_r = r["z_s"], r["z_r"]

    def z_copy(k):
        return remote("zs", z_s.at[k], z_r.at[z], k, z, at(k, x, core, y))

    def z_step(j, carry):
        k = lax.rem(z + n_z // 2 + j, n_z)
        core_copy(k).wait_recv()
        z_s[k] = (halves[k, core] + core_r[k].astype(F32)).astype(BF16)

        @pl.when(k != z)
        def _():
            z_copy(k).start()

        return carry

    lax.fori_loop(0, n_z, z_step, 0)
    pending.append(lambda: each("z", lambda p, me, device: z_copy(p).wait_send()))
    own = halves[z, core] + core_r[z].astype(F32)

    part_units = units // n_x
    mine_units = pl.ds(pl.multiple_of(x * part_units, part_units), part_units)
    before = preact_x[:, :, mine_units].astype(F32).reshape(line_rows, part_units)
    hidden_x = (before / (1.0 + jnp.exp(-before))).astype(BF16)
    er_s, er_r, eb, ex = r["er_s"], r["er_r"], r["eb"], r["ex"]
    er_s[...] = (
        tn(hidden_x, grad_x[...].reshape(line_rows, emb)).astype(BF16).reshape(er_s.shape)
    )
    send("er", "b", lambda p: er_s.at[p], lambda me: er_r.at[me])
    er_r[b] = er_s[b]
    feats_part(1)
    feats_part(2)
    receive("er", "b", lambda p: er_r.at[p])
    eb[b] = jnp.sum(er_r[...].astype(F32), axis=0).astype(BF16)
    send("eb", "b", lambda p: eb.at[b], lambda me: eb.at[me])
    feats_part(3)

    shifts = third("e5", True)

    def item_part(j, carry):
        notes = info[rows_of(j), :]
        block_in, used_in = notes[:, 0:1], notes[:, 1:2]
        bits = chunk_of(shifts, j).astype(F32)
        shift_in = bits[:, 0:1] + bits[:, 1:2] + bits[:, 2:3]
        valid_in = iota((chunk_rows, BLK), 1).astype(F32) < used_in
        student = jnp.where(valid_in, jnp.exp(scores[rows_of(j), :] - shift_in), 0.0)
        spread[rows_of(j), :] = lift(student - teacher_n[rows_of(j), :], block_in)
        return carry

    lax.fori_loop(0, chunks, item_part, 0)

    def item_block(j, carry):
        columns = pl.ds(pl.multiple_of(j * 256, 256), 256)
        r["grad_items"][columns, :] = tn(
            spread[:, columns], queries[...].reshape(rows, emb)
        )
        return carry

    lax.fori_loop(0, BLK_DEV * BLK // 256, item_block, 0)
    receive("eb", "b", lambda p: eb.at[p])
    ex[x] = eb[...].reshape(part_units, emb)
    send("ex", "x", lambda p: ex.at[x], lambda me: ex.at[me])
    for part in range(4):
        columns = pl.ds(part * (depth // 4), depth // 4)
        receive("gf" + str(part), "y", lambda p: gf_r.at[p, :, columns])
    gf_r[y] = gf_s[y]
    r["grad_feats"][...] = jnp.sum(gf_r[...].astype(F32), axis=0)
    receive("ex", "x", lambda p: ex.at[p])
    r["grad_embed"][...] = ex[...].astype(F32).reshape(units, emb)
    each(
        "z",
        lambda p, me, device: remote(
            "zs", z_r.at[p], z_r.at[p], p, p, device(p)
        ).wait_recv(),
    )
    z_r[z] = jnp.zeros((half, units), BF16)
    r["grad_hidden"][...] = own + jnp.sum(z_r[...].astype(F32), axis=0)
    for finish in pending:
        finish()


def per_device(
    n_z, n_x, n_y, feats, w_hidden, w_embed, items, teacher, block_counts, tail_rows,
    cand_owner, cand_block,
):
    q_dev, depth = feats.shape
    units, emb = w_embed.shape
    slots = cand_owner.shape[0]
    n_a, n_b = n_x * n_y, n_z * 2
    rows = n_a * n_b * CAP
    group_rows = n_y * q_dev
    block_cols = depth // (n_z * n_x)
    half = block_cols // 2
    part_units = units // n_x
    inputs = {
        "feats": feats,
        "w_hidden": w_hidden,
        "w_embed": w_embed,
        "items": items,
        "teacher": teacher,
        "counts": block_counts,
        "tails": tail_rows.reshape(1, q_dev),
        "owner": cand_owner,
        "owner_row": cand_owner.reshape(1, slots),
        "block": cand_block.reshape(slots, 1),
    }
    outputs = {
        "grad_feats": (q_dev, depth),
        "grad_hidden": (half, units),
        "grad_embed": (units, emb),
        "grad_items": (BLK_DEV * BLK, emb),
    }
    vmem = {
        "weights": ((depth, units), BF16),
        "feats_y": ((n_y, q_dev, depth), BF16),
        "perm": ((rows, rows), BF16),
        "member_row": ((rows, q_dev), F32),
        "preact": ((group_rows, units), F32),
        "preact_x": ((n_x, group_rows, units), BF16),
        "emb_s": ((n_y, q_dev, emb), F32),
        "emb_r": ((n_y, q_dev, emb), F32),
        "teacher_n": ((rows, BLK), F32),
        "info": ((rows, 128), F32),
        "spread": ((rows, BLK_DEV * BLK), BF16),
        "feats_s": ((n_x, group_rows, n_z * block_cols), BF16),
        "feats_x": ((n_x, group_rows, n_z * block_cols), BF16),
        "scores": ((rows, BLK), F32),
        "grad_y": ((n_y, q_dev, emb), BF16),
        "grad_x": ((n_x, group_rows, emb), BF16),
        "gf_s": ((n_y, q_dev, depth), BF16),
        "gf_r": ((n_y, q_dev, depth), BF16),
        "pre_x": ((n_x, group_rows, units), BF16),
        "halves": ((n_z, 2, half, units), F32),
        "halves_bf": ((n_z, 2, half, units), BF16),
        "core_r": ((n_z, half, units), BF16),
        "z_s": ((n_z, half, units), BF16),
        "z_r": ((n_z, half, units), BF16),
        "er_s": ((n_b, part_units // n_b, emb), BF16),
        "er_r": ((n_b, part_units // n_b, emb), BF16),
        "eb": ((n_b, part_units // n_b, emb), BF16),
        "ex": ((n_x, part_units, emb), BF16),
    }
    for name, lanes, ahead in (
        ("e1", 256, True),
        ("e2", emb, False),
        ("e3", emb, True),
        ("e4", emb + 128, False),
        ("e5", 128, True),
    ):
        one, two = ((n_a, 2 * n_b, lanes), (n_b, 2 * n_a, lanes))
        if not ahead:
            one, two = two, one
        for suffix, shape in (("_s1", one), ("_r1", one), ("_s2", two), ("_r2", two)):
            vmem[name + suffix] = (shape, BF16)
    scratch = [pltpu.VMEM(shape, kind) for shape, kind in vmem.values()]
    most = max(n_a, n_b)
    scratch += [
        pltpu.SemaphoreType.DMA((len(STAGES), most)),
        pltpu.SemaphoreType.DMA((len(STAGES), most)),
        pltpu.SemaphoreType.DMA,
    ]
    names = list(inputs) + list(outputs) + list(vmem) + ["send_sem", "recv_sem", "load_sem"]
    specs = [
        pl.BlockSpec(memory_space=pl.ANY if name == "w_hidden" else pltpu.VMEM)
        for name in inputs
    ]
    return pl.pallas_call(
        functools.partial(kernel, n_z, n_x, n_y, names),
        out_shape=[jax.ShapeDtypeStruct(shape, F32) for shape in outputs.values()],
        in_specs=specs,
        out_specs=[pl.BlockSpec(memory_space=pltpu.VMEM)] * len(outputs),
        scratch_shapes=scratch,
        compiler_params=pltpu.CompilerParams(
            collective_id=0, has_side_effects=True, vmem_limit_bytes=58 * 1024 * 1024
        ),
    )(*inputs.values())


def solution(mesh):
    n_y = mesh.shape["sub"]
    n_x = n_y
    n_z = mesh.shape["shard"] // (2 * n_x)
    both = ("shard", "sub")
    placed = (
        P(both, None),
        P(None, "sub"),
        P("sub", None),
        P(both, None),
        P(both, None),
        P(both, None),
        P(both),
        P(both, None),
        P(both),
    )
    return jax.shard_map(
        functools.partial(per_device, n_z, n_x, n_y),
        mesh=mesh,
        in_specs=placed,
        out_specs=(P(both, None), P("shard", "sub"), P("sub", None), P(both, None)),
        check_vma=False,
    )
```

time: 588 us -> 161 us (0.27)
  waiting for transfers between devices: 337 us -> 0 us
  Pallas kernels: 0 us -> 149 us
  starting transfers between devices: 77.6 us -> 0 us
  blocking collectives: 60 us -> 0 us
  other arithmetic: 31.5 us -> 0 us
  matrix products: 30.4 us -> 0 us
  local copies, waits for them, and re-layouts: 36 us -> 11 us
  between operations: 14.3 us -> 0.64 us
    unnamed x5 -> x0, waiting for transfers between devices: 201 us -> none
    pallas_call x0 -> x1, Pallas kernels: none -> 149 us  [per_device(): pl.pallas_call(functools.partial(kernel, n_z, n_x, n_y, names), out_shape...]
    all_to_all x14 -> x0, waiting for transfers between devices: 106 us -> none  [the longest x7 73.4 us: exchange(): lax.all_to_all(array, 'shard', split_axis=0, concat_axis=0, tiled=True)]
    all_to_all x14 -> x0, starting transfers between devices: 77.5 us -> none  [the longest x7 53.9 us: exchange(): lax.all_to_all(array, 'shard', split_axis=0, concat_axis=0, tiled=True)]
    all_gather x2 -> x0, blocking collectives: 60 us -> none  [the longest x1 50.8 us: per_device(): lax.all_gather(embed_part, 'shard', axis=0, tiled=True).astype(F32)]
    dot_general x15 -> x0, matrix products: 30.4 us -> none  [dot(): lax.dot_general(left, right, ((dims[0], dims[1]), ((), ())), precision=pr...]
    reduce_scatter x2 -> x0, waiting for transfers between devices: 17.6 us -> none  [the longest x1 17.6 us: per_device(): lax.psum_scatter(nn(hidden, w_embed), 'sub', scatter_dimension=0, tiled=T...]
    all_gather x1 -> x0, waiting for transfers between devices: 12.2 us -> none  [per_device(): gathered = lax.all_gather(feats, 'sub', axis=0, tiled=True)]
  transfers between devices with their start and end apart: 18 -> 0, of which waited for: 15 -> 0; matrix products, arithmetic and copies ran while one was open for 11% -> 0% of each run, Pallas kernels for 0% -> 0%
where the time goes in v2:
time: 161 us
  Pallas kernels  149 us (93%)
  local copies, waits for them, and re-layouts  11 us (7%)
    pallas_call x1, Pallas kernels, per_device(): pl.pallas_call(functools.partial(kernel, n_z, n_x, n_y, names), out_shape...  149 us
    unnamed x5, local copies, waits for them, and re-layouts  9.53 us

profile of v2, /device:TPU:1, one launch (start us, length us, event | category | flops | bytes accessed | tf_op | source)
XLA Modules:
  0.0 160.6 jit_solution(13223864518983241337)
XLA Ops:
  0.6 1.5 copy.15.refs_9_
  2.1 1.5 copy.14.refs_7_
  3.6 149.0 %shard_map.120 = (f32[32,4096]{1,0:T(8,128)}, f32[64,1024]{1,0:T(8,128)}, f32[1024,256]{1,0:T(8,128)}, f32[1024,256]{1,0:T(8,128)}) custom-call(bf16[32,4096]{1,0:T(8,128)(2,1)} %refs_0_.1, bf16[4096,1024]{1,0:T(8,128)(2,1)} %refs_1_.1, bf16[1024,256]{1,0:T(8,128)(2,1)} %refs_2_.1, bf16[1024,256]{1,0:T(8,128)(2,1)} %refs_3_.1, bf16[256,128]{1,0:T(8,128)(2,1)} %refs_4_.1, ...), custom_call_target="tpu_custom_call" | custom-call | tf_op jit(solution)/shard_map/pallas_call | solution.py:589
  152.5 1.9 %copy.20 = f32[32,4096]{1,0:T(8,128)} copy(f32[32,4096]{1,0:T(8,128)} %get-tuple-element.8) | data formatting | bytes 1048576
  154.4 1.7 %copy.21 = f32[64,1024]{1,0:T(8,128)} copy(f32[64,1024]{1,0:T(8,128)} %get-tuple-element.9) | data formatting | bytes 524288
  156.1 2.3 %copy.22 = f32[1024,256]{1,0:T(8,128)} copy(f32[1024,256]{1,0:T(8,128)} %get-tuple-element.10) | data formatting | bytes 2097152
  158.3 2.3 %copy.23 = f32[1024,256]{1,0:T(8,128)} copy(f32[1024,256]{1,0:T(8,128)} %get-tuple-element.11) | data formatting | bytes 2097152

commit v3 on v2

--- a/solution.py
+++ b/solution.py
@@ -17,7 +17,7 @@
 MESH = pl.DeviceIdType.MESH
 STAGES = (
     "feats", "emb", "e1a", "e1b", "e2b", "e2a", "e3a", "e3b", "e4b", "e4a", "e5a", "e5b",
-    "px", "fx", "gy", "gx", "core", "zs", "gf0", "gf1", "gf2", "gf3", "er", "eb", "ex",
+    "px", "fx", "ga", "core", "zs", "gf0", "gf1", "gf2", "gf3", "er", "eb", "ex",
 )
 
 
@@ -143,8 +143,6 @@
         )
     feats_y = r["feats_y"]
     feats_y[y] = feats[...]
-    pl.semaphore_wait(barrier, n_a + n_b - 2)
-    send("feats", "y", lambda p: feats, lambda me: feats_y.at[me])
 
     perm = r["perm"]
     log_a, log_b = n_a.bit_length() - 1, n_b.bit_length() - 1
@@ -202,9 +200,16 @@
     total = jnp.sum(jnp.where(member, slot_sum, 0.0), axis=0, keepdims=True)
     query_shift = query_top + jnp.log(total / n_cand)
     slot_shift = jnp.sum(jnp.where(member, query_shift, 0.0), axis=1, keepdims=True)
-    owner = r["owner"][...]
+    diagonal = iota((slots, slots), 0) == iota((slots, slots), 1)
+    owner_row = r["owner"][...]
+    owner = jnp.sum(
+        jnp.where(diagonal, owner_row.astype(F32), 0.0), axis=1, keepdims=True
+    ).astype(I32)
+    block = jnp.sum(
+        jnp.where(diagonal, r["block"][...].astype(F32), 0.0), axis=1, keepdims=True
+    )
     same = jnp.logical_and(
-        r["owner_row"][...] == owner, iota((slots, slots), 1) < iota((slots, slots), 0)
+        owner_row == owner, iota((slots, slots), 1) < iota((slots, slots), 0)
     )
     rank = jnp.sum(jnp.where(same, 1.0, 0.0), axis=1, keepdims=True)
     log_y, log_x = n_y.bit_length() - 1, n_x.bit_length() - 1
@@ -215,13 +220,16 @@
     base = ((owner_x * n_y + owner_y) * n_b + owner_z * 2 + owner_core) * CAP
     dest = base.astype(F32) + rank
     place = jnp.where(dest == iota((slots, rows), 1).astype(F32), 1.0, 0.0).astype(BF16)
-    side = in_lanes((r["block"][...].astype(F32), slot_used) + pieces(slot_shift), slots)
+    side = in_lanes((block, slot_used) + pieces(slot_shift), slots)
     payload = jnp.concatenate([logit, side], axis=1).astype(BF16)
-    r["e1_s1"][...] = tn(place, payload).astype(BF16).reshape(r["e1_s1"].shape)
-    first("e1", True)
+    placed = tn(place, payload).astype(BF16)
+    r["e1_s1"][...] = nn(perm[...], placed).astype(BF16).reshape(r["e1_s1"].shape)
     member_row = r["member_row"]
     member_row[...] = tn(place, jnp.where(member, 1.0, 0.0).astype(BF16))
-    second("e1", True)
+    pl.semaphore_wait(barrier, n_a + n_b - 2)
+    send("feats", "y", lambda p: feats, lambda me: feats_y.at[me])
+    first("e1", False)
+    second("e1", False)
 
     receive("feats", "y", lambda p: feats_y.at[p])
     load.wait()
@@ -253,7 +261,9 @@
         parts = [jnp.where(block_in == float(k), values, 0.0).astype(BF16) for k in range(BLK_DEV)]
         return jnp.concatenate(parts, axis=1)
 
-    sent = third("e1", True)
+    sent = r["e1_q"]
+    by_owner = third("e1", False)[...].reshape(rows, 2 * BLK)
+    sent[...] = nn(perm[...], by_owner).astype(BF16).reshape(sent.shape)
     teacher_n, info, spread = r["teacher_n"], r["info"], r["spread"]
 
     def chunk_of(ref, j):
@@ -285,7 +295,9 @@
     member_bf = member_row[...].astype(BF16)
     r["e3_s1"][...] = nn(member_bf, query_emb).astype(BF16).reshape(r["e3_s1"].shape)
     first("e3", True)
+
     second("e2", False)
+    second("e3", True)
     preact_x[x] = preact[...].astype(BF16)
     feats_s, feats_x = r["feats_s"], r["feats_x"]
     for p in range(n_x):
@@ -294,12 +306,9 @@
             feats_s[p, :, k * block_cols : (k + 1) * block_cols] = feats_y[
                 :, :, column : column + block_cols
             ].reshape(group_rows, block_cols)
-    second("e3", True)
     send("px", "x", lambda p: preact_x.at[x], lambda me: preact_x.at[me])
     send("fx", "x", lambda p: feats_s.at[p], lambda me: feats_x.at[me])
     feats_x[x] = feats_s[x]
-    back = third("e2", False)
-    query_teacher = tn(member_bf, back[...].reshape(rows, emb))
 
     queries = third("e3", True)
     scores = r["scores"]
@@ -326,6 +335,8 @@
     lax.fori_loop(0, chunks, score_part, 0)
     first("e4", False)
     second("e4", False)
+    back = third("e2", False)
+    query_teacher = tn(member_bf, back[...].reshape(rows, emb))
     returned = third("e4", False)[...].reshape(rows, emb + 128)
 
     lse_bits = returned[:, emb : emb + 128].astype(F32)
@@ -346,21 +357,92 @@
             - emb_raw * inv_rms * inv_rms * jnp.mean(gradient * emb_raw, axis=1, keepdims=True)
         )
     ).astype(BF16)
-    grad_y, grad_x = r["grad_y"], r["grad_x"]
-    grad_y[y] = grad_emb
-    send("gy", "y", lambda p: grad_y.at[y], lambda me: grad_y.at[me])
+    grad_a = r["grad_a"]
+    grad_a[a] = grad_emb
+    send("ga", "a", lambda p: grad_a.at[a], lambda me: grad_a.at[me])
     shift = query_max - jnp.log(scale)
     row_shift = jnp.sum(jnp.where(mine, shift, 0.0), axis=1, keepdims=True)
     r["e5_s1"][...] = in_lanes(pieces(row_shift), rows).astype(BF16).reshape(r["e5_s1"].shape)
     first("e5", True)
-    receive("gy", "y", lambda p: grad_y.at[p])
-    grad_group = grad_y[...].reshape(group_rows, emb)
-    grad_x[x] = grad_group
-    send("gx", "x", lambda p: grad_x.at[x], lambda me: grad_x.at[me])
-
     def derivative(dhidden, before):
         sig = 1.0 / (1.0 + jnp.exp(-before))
         return (dhidden * sig * (1.0 + before * (1.0 - sig))).astype(BF16)
+
+    receive("px", "x", lambda p: preact_x.at[p])
+    receive("fx", "x", lambda p: feats_x.at[p])
+    receive("ga", "a", lambda p: grad_a.at[p])
+    second("e5", True)
+    grad_group = grad_a[pl.ds(x * n_y, n_y)].reshape(group_rows, emb)
+
+    pre_x = r["pre_x"]
+
+    def pre_part(j, carry):
+        part = grad_a[pl.ds(j * n_y, n_y)].reshape(group_rows, emb)
+        pre_x[j] = derivative(nt(part, w_embed[...]), preact_x[j].astype(F32))
+        return carry
+
+    lax.fori_loop(0, n_x, pre_part, 0)
+    line_rows = n_x * group_rows
+
+    part_units = units // n_x
+    mine_units = pl.ds(pl.multiple_of(x * part_units, part_units), part_units)
+    before = preact_x[:, :, mine_units].astype(F32).reshape(line_rows, part_units)
+    hidden_x = (before / (1.0 + jnp.exp(-before))).astype(BF16)
+    er_s, er_r, eb, ex = r["er_s"], r["er_r"], r["eb"], r["ex"]
+    er_s[...] = tn(hidden_x, grad_a[...].reshape(line_rows, emb)).astype(BF16).reshape(er_s.shape)
+    send("er", "b", lambda p: er_s.at[p], lambda me: er_r.at[me])
+    er_r[b] = er_s[b]
+
+    halves, halves_bf, core_r = r["halves"], r["halves_bf"], r["core_r"]
+    z_s, z_r = r["z_s"], r["z_r"]
+    mate = at(z, x, 1 - core, y)
+
+    def core_copy(k):
+        return remote("core", halves_bf.at[k, 1 - core], core_r.at[k], k, k, mate)
+
+    def z_copy(k):
+        return remote("zs", z_s.at[k], z_r.at[z], k, z, at(k, x, core, y))
+
+    def block_at(j):
+        return lax.rem(z + n_z // 2 + j, n_z)
+
+    def hidden_part(j):
+        k = block_at(j)
+        columns = pl.ds(pl.multiple_of(k * block_cols, block_cols), block_cols)
+        left = feats_x[:, :, columns].reshape(line_rows, block_cols)
+        value = tn(left, pre_x[...].reshape(line_rows, units)).reshape(2, half, units)
+        halves[k] = value
+        halves_bf[k] = value.astype(BF16)
+        core_copy(k).start()
+
+    def z_part(j):
+        k = block_at(j)
+        core_copy(k).wait_recv()
+        z_s[k] = (halves[k, core] + core_r[k].astype(F32)).astype(BF16)
+
+        @pl.when(k != z)
+        def _():
+            z_copy(k).start()
+
+    lead = n_z // 2
+    for j in range(lead):
+        hidden_part(j)
+    receive("er", "b", lambda p: er_r.at[p])
+    eb[b] = jnp.sum(er_r[...].astype(F32), axis=0).astype(BF16)
+    send("eb", "b", lambda p: eb.at[b], lambda me: eb.at[me])
+
+    def both_parts(j, carry):
+        z_part(j)
+        hidden_part(j + lead)
+        return carry
+
+    lax.fori_loop(0, n_z - lead, both_parts, 0)
+    lax.fori_loop(n_z - lead, n_z, lambda j, carry: (z_part(j), carry)[1], 0)
+    pending.append(
+        lambda: lax.fori_loop(0, n_z, lambda k, s: (core_copy(k).wait_send(), s)[1], 0)
+    )
+    pending.append(lambda: each("z", lambda p, me, device: z_copy(p).wait_send()))
+    own = halves[z, core] + core_r[z].astype(F32)
 
     grad_pre = derivative(nt(grad_group, w_embed[...]), preact[...])
     gf_s, gf_r = r["gf_s"], r["gf_r"]
@@ -385,77 +467,11 @@
             lambda p: gf_s.at[p, :, columns],
             lambda me: gf_r.at[me, :, columns],
         )
-
-    feats_part(0)
-    second("e5", True)
-    receive("px", "x", lambda p: preact_x.at[p])
-    receive("fx", "x", lambda p: feats_x.at[p])
-    receive("gx", "x", lambda p: grad_x.at[p])
-
-    pre_x = r["pre_x"]
-
-    def pre_part(j, carry):
-        pre_x[j] = derivative(nt(grad_x[j], w_embed[...]), preact_x[j].astype(F32))
-        return carry
-
-    lax.fori_loop(0, n_x, pre_part, 0)
-    line_rows = n_x * group_rows
-    halves, halves_bf, core_r = r["halves"], r["halves_bf"], r["core_r"]
-    mate = at(z, x, 1 - core, y)
-
-    def core_copy(k):
-        return remote("core", halves_bf.at[k, 1 - core], core_r.at[k], k, k, mate)
-
-    def hidden_part(j, carry):
-        k = lax.rem(z + n_z // 2 + j, n_z)
-        columns = pl.ds(pl.multiple_of(k * block_cols, block_cols), block_cols)
-        left = feats_x[:, :, columns].reshape(line_rows, block_cols)
-        value = tn(left, pre_x[...].reshape(line_rows, units)).reshape(2, half, units)
-        halves[k] = value
-        halves_bf[k] = value.astype(BF16)
-        core_copy(k).start()
-        return carry
-
-    lax.fori_loop(0, n_z, hidden_part, 0)
-    pending.append(
-        lambda: lax.fori_loop(0, n_z, lambda k, s: (core_copy(k).wait_send(), s)[1], 0)
-    )
-    z_s, z_r = r["z_s"], r["z_r"]
-
-    def z_copy(k):
-        return remote("zs", z_s.at[k], z_r.at[z], k, z, at(k, x, core, y))
-
-    def z_step(j, carry):
-        k = lax.rem(z + n_z // 2 + j, n_z)
-        core_copy(k).wait_recv()
-        z_s[k] = (halves[k, core] + core_r[k].astype(F32)).astype(BF16)
-
-        @pl.when(k != z)
-        def _():
-            z_copy(k).start()
-
-        return carry
-
-    lax.fori_loop(0, n_z, z_step, 0)
-    pending.append(lambda: each("z", lambda p, me, device: z_copy(p).wait_send()))
-    own = halves[z, core] + core_r[z].astype(F32)
-
-    part_units = units // n_x
-    mine_units = pl.ds(pl.multiple_of(x * part_units, part_units), part_units)
-    before = preact_x[:, :, mine_units].astype(F32).reshape(line_rows, part_units)
-    hidden_x = (before / (1.0 + jnp.exp(-before))).astype(BF16)
-    er_s, er_r, eb, ex = r["er_s"], r["er_r"], r["eb"], r["ex"]
-    er_s[...] = (
-        tn(hidden_x, grad_x[...].reshape(line_rows, emb)).astype(BF16).reshape(er_s.shape)
-    )
-    send("er", "b", lambda p: er_s.at[p], lambda me: er_r.at[me])
-    er_r[b] = er_s[b]
-    feats_part(1)
-    feats_part(2)
-    receive("er", "b", lambda p: er_r.at[p])
-    eb[b] = jnp.sum(er_r[...].astype(F32), axis=0).astype(BF16)
-    send("eb", "b", lambda p: eb.at[b], lambda me: eb.at[me])
-    feats_part(3)
+    for part in range(4):
+        feats_part(part)
+    receive("eb", "b", lambda p: eb.at[p])
+    ex[x] = eb[...].reshape(part_units, emb)
+    send("ex", "x", lambda p: ex.at[x], lambda me: ex.at[me])
 
     shifts = third("e5", True)
 
@@ -479,9 +495,6 @@
         return carry
 
     lax.fori_loop(0, BLK_DEV * BLK // 256, item_block, 0)
-    receive("eb", "b", lambda p: eb.at[p])
-    ex[x] = eb[...].reshape(part_units, emb)
-    send("ex", "x", lambda p: ex.at[x], lambda me: ex.at[me])
     for part in range(4):
         columns = pl.ds(part * (depth // 4), depth // 4)
         receive("gf" + str(part), "y", lambda p: gf_r.at[p, :, columns])
@@ -499,6 +512,12 @@
     r["grad_hidden"][...] = own + jnp.sum(z_r[...].astype(F32), axis=0)
     for finish in pending:
         finish()
+
+
+def hand_on(*refs):
+    count = len(refs) // 2
+    for k in range(count):
+        refs[count + k][...] = refs[k][...]
 
 
 def per_device(
@@ -522,9 +541,8 @@
         "teacher": teacher,
         "counts": block_counts,
         "tails": tail_rows.reshape(1, q_dev),
-        "owner": cand_owner,
-        "owner_row": cand_owner.reshape(1, slots),
-        "block": cand_block.reshape(slots, 1),
+        "owner": cand_owner.reshape(1, slots),
+        "block": cand_block.reshape(1, slots),
     }
     outputs = {
         "grad_feats": (q_dev, depth),
@@ -547,8 +565,8 @@
         "feats_s": ((n_x, group_rows, n_z * block_cols), BF16),
         "feats_x": ((n_x, group_rows, n_z * block_cols), BF16),
         "scores": ((rows, BLK), F32),
-        "grad_y": ((n_y, q_dev, emb), BF16),
-        "grad_x": ((n_x, group_rows, emb), BF16),
+        "e1_q": ((n_b, 2 * n_a, 2 * BLK), BF16),
+        "grad_a": ((n_a, q_dev, emb), BF16),
         "gf_s": ((n_y, q_dev, depth), BF16),
         "gf_r": ((n_y, q_dev, depth), BF16),
         "pre_x": ((n_x, group_rows, units), BF16),
@@ -563,7 +581,7 @@
         "ex": ((n_x, part_units, emb), BF16),
     }
     for name, lanes, ahead in (
-        ("e1", 256, True),
+        ("e1", 256, False),
         ("e2", emb, False),
         ("e3", emb, True),
         ("e4", emb + 128, False),
@@ -586,7 +604,7 @@
         pl.BlockSpec(memory_space=pl.ANY if name == "w_hidden" else pltpu.VMEM)
         for name in inputs
     ]
-    return pl.pallas_call(
+    results = pl.pallas_call(
         functools.partial(kernel, n_z, n_x, n_y, names),
         out_shape=[jax.ShapeDtypeStruct(shape, F32) for shape in outputs.values()],
         in_specs=specs,
@@ -596,6 +614,12 @@
             collective_id=0, has_side_effects=True, vmem_limit_bytes=58 * 1024 * 1024
         ),
     )(*inputs.values())
+    return pl.pallas_call(
+        hand_on,
+        out_shape=[jax.ShapeDtypeStruct(shape, F32) for shape in outputs.values()],
+        in_specs=[pl.BlockSpec(memory_space=pltpu.VMEM)] * len(outputs),
+        out_specs=[pl.BlockSpec(memory_space=pltpu.VMEM)] * len(outputs),
+    )(*results)
 
 
 def solution(mesh):

time: 161 us -> 134 us (0.83)
  Pallas kernels: 149 us -> 133 us
  local copies, waits for them, and re-layouts: 11 us -> 0 us
    pallas_call x1, Pallas kernels: 149 us -> 130 us  [per_device(): pl.pallas_call(functools.partial(kernel, n_z, n_x, n_y, names), out_shape...]
    unnamed x5 -> x0, local copies, waits for them, and re-layouts: 9.53 us -> none
    pallas_call x0 -> x1, Pallas kernels: none -> 3.38 us  [per_device(): pl.pallas_call(hand_on, out_shape=[jax.ShapeDtypeStruct(shape, F32) for s...]
where the time goes in v3:
time: 134 us
  Pallas kernels  133 us (99%)
    pallas_call x1, Pallas kernels, per_device(): pl.pallas_call(functools.partial(kernel, n_z, n_x, n_y, names), out_shape...  130 us
    pallas_call x1, Pallas kernels, per_device(): pl.pallas_call(hand_on, out_shape=[jax.ShapeDtypeStruct(shape, F32) for s...  3.38 us

profile of v3, /device:TPU:1, one launch (start us, length us, event | category | flops | bytes accessed | tf_op | source)
XLA Modules:
  0.0 134.0 jit_solution(4048596770964483273)
XLA Ops:
  0.6 130.0 %shard_map.120 = (f32[32,4096]{1,0:T(8,128)}, f32[64,1024]{1,0:T(8,128)}, f32[1024,256]{1,0:T(8,128)}, f32[1024,256]{1,0:T(8,128)}) custom-call(bf16[32,4096]{1,0:T(8,128)(2,1)} %refs_0_.1, bf16[4096,1024]{1,0:T(8,128)(2,1)} %refs_1_.1, bf16[1024,256]{1,0:T(8,128)(2,1)} %refs_2_.1, bf16[1024,256]{1,0:T(8,128)(2,1)} %refs_3_.1, bf16[256,128]{1,0:T(8,128)(2,1)} %refs_4_.1, ...), custom_call_target="tpu_custom_call" | custom-call | tf_op jit(solution)/shard_map/pallas_call | solution.py:607
  130.6 3.4 %shard_map.121 = (f32[32,4096]{1,0:T(8,128)}, f32[64,1024]{1,0:T(8,128)}, f32[1024,256]{1,0:T(8,128)}, f32[1024,256]{1,0:T(8,128)}) custom-call(f32[32,4096]{1,0:T(8,128)} %get-tuple-element.8.refs_0_, f32[64,1024]{1,0:T(8,128)} %get-tuple-element.9.refs_1_, f32[1024,256]{1,0:T(8,128)} %get-tuple-element.10.refs_2_, f32[1024,256]{1,0:T(8,128)} %get-tuple-element.11.refs_3_), custom_call_target="tpu_custom_call" | custom-call | tf_op jit(solution)/shard_map/pallas_call | solution.py:617

commit v4 on v3

--- a/solution.py
+++ b/solution.py
@@ -108,27 +108,22 @@
             body(lax.rem(me + j, size), me, device)
             return carry
 
-        lax.fori_loop(1, size, step, 0)
+        lax.fori_loop(1, size, step, 0, unroll=True)
+
+    def whole(stage, group, target):
+        size, me, device = groups[group]
+        others = target(pl.ds(0, size - 1))
+        return remote(stage, others, others, 0, 0, device(lax.rem(me + 1, size)))
 
     def send(stage, group, source, target):
         def start(p, me, device):
-            remote(stage, source(p), target(me), p, me, device(p)).start()
+            remote(stage, source(p), target(me), 0, 0, device(p)).start()
 
         each(group, start)
-
-        def finish():
-            def wait(p, me, device):
-                remote(stage, source(p), target(me), p, me, device(p)).wait_send()
-
-            each(group, wait)
-
-        pending.append(finish)
+        pending.append(lambda: whole(stage, group, target).wait_send())
 
     def receive(stage, group, target):
-        def wait(p, me, device):
-            remote(stage, target(p), target(p), p, p, device(p)).wait_recv()
-
-        each(group, wait)
+        whole(stage, group, target).wait_recv()
 
     weights = r["weights"]
     load = pltpu.make_async_copy(w_hbm, weights, r["load_sem"])
@@ -313,7 +308,10 @@
     queries = third("e3", True)
     scores = r["scores"]
 
-    def score_part(j, carry):
+    e4_s, e4_r = r["e4_s1"], r["e4_r1"]
+
+    def score_part(turn, carry):
+        j = lax.rem(turn + b // per + 1, chunks)
         every = nt(chunk_of(queries, j), items[...])
         notes = info[rows_of(j), :]
         block_in, used_in = notes[:, 0:1], notes[:, 1:2]
@@ -329,11 +327,19 @@
         empty = used_in < 0.5
         lse = jnp.where(empty, 0.0, row_top + jnp.log(row_sum))
         message = jnp.concatenate([term, in_lanes(pieces(lse), chunk_rows)], axis=1)
-        r["e4_s1"][pl.ds(j * per, per)] = message.astype(BF16).reshape(per, 2 * n_a, emb + 128)
+        e4_s[pl.ds(j * per, per)] = message.astype(BF16).reshape(per, 2 * n_a, emb + 128)
+        for i in range(per):
+            p = j * per + i
+
+            @pl.when(p != b)
+            def _():
+                remote("e4b", e4_s.at[p], e4_r.at[b], 0, 0, groups["b"][2](p)).start()
+
         return carry
 
     lax.fori_loop(0, chunks, score_part, 0)
-    first("e4", False)
+    pending.append(lambda: whole("e4b", "b", lambda p: e4_r.at[p]).wait_send())
+    e4_r[b] = e4_s[b]
     second("e4", False)
     back = third("e2", False)
     query_teacher = tn(member_bf, back[...].reshape(rows, emb))
@@ -371,7 +377,6 @@
     receive("px", "x", lambda p: preact_x.at[p])
     receive("fx", "x", lambda p: feats_x.at[p])
     receive("ga", "a", lambda p: grad_a.at[p])
-    second("e5", True)
     grad_group = grad_a[pl.ds(x * n_y, n_y)].reshape(group_rows, emb)
 
     pre_x = r["pre_x"]
@@ -398,10 +403,10 @@
     mate = at(z, x, 1 - core, y)
 
     def core_copy(k):
-        return remote("core", halves_bf.at[k, 1 - core], core_r.at[k], k, k, mate)
+        return remote("core", halves_bf.at[k, 1 - core], core_r.at[k], 0, k, mate)
 
     def z_copy(k):
-        return remote("zs", z_s.at[k], z_r.at[z], k, z, at(k, x, core, y))
+        return remote("zs", z_s.at[k], z_r.at[z], 0, 0, at(k, x, core, y))
 
     def block_at(j):
         return lax.rem(z + n_z // 2 + j, n_z)
@@ -427,6 +432,7 @@
     lead = n_z // 2
     for j in range(lead):
         hidden_part(j)
+    second("e5", True)
     receive("er", "b", lambda p: er_r.at[p])
     eb[b] = jnp.sum(er_r[...].astype(F32), axis=0).astype(BF16)
     send("eb", "b", lambda p: eb.at[b], lambda me: eb.at[me])
@@ -439,9 +445,9 @@
     lax.fori_loop(0, n_z - lead, both_parts, 0)
     lax.fori_loop(n_z - lead, n_z, lambda j, carry: (z_part(j), carry)[1], 0)
     pending.append(
-        lambda: lax.fori_loop(0, n_z, lambda k, s: (core_copy(k).wait_send(), s)[1], 0)
-    )
-    pending.append(lambda: each("z", lambda p, me, device: z_copy(p).wait_send()))
+        lambda: remote("core", core_r, core_r, 0, 0, mate).wait_send()
+    )
+    pending.append(lambda: whole("zs", "z", lambda p: z_r.at[p]).wait_send())
     own = halves[z, core] + core_r[z].astype(F32)
 
     grad_pre = derivative(nt(grad_group, w_embed[...]), preact[...])
@@ -502,12 +508,7 @@
     r["grad_feats"][...] = jnp.sum(gf_r[...].astype(F32), axis=0)
     receive("ex", "x", lambda p: ex.at[p])
     r["grad_embed"][...] = ex[...].astype(F32).reshape(units, emb)
-    each(
-        "z",
-        lambda p, me, device: remote(
-            "zs", z_r.at[p], z_r.at[p], p, p, device(p)
-        ).wait_recv(),
-    )
+    receive("zs", "z", lambda p: z_r.at[p])
     z_r[z] = jnp.zeros((half, units), BF16)
     r["grad_hidden"][...] = own + jnp.sum(z_r[...].astype(F32), axis=0)
     for finish in pending:
@@ -515,9 +516,22 @@
 
 
 def hand_on(*refs):
-    count = len(refs) // 2
-    for k in range(count):
-        refs[count + k][...] = refs[k][...]
+    count = (len(refs) - 2) // 3
+    sources, targets, buffers = refs[:count], refs[count : 2 * count], refs[2 * count : 3 * count]
+    load_sem, store_sem = refs[-2:]
+    loads = [
+        pltpu.make_async_copy(sources[k], buffers[k], load_sem.at[k]) for k in range(count)
+    ]
+    stores = [
+        pltpu.make_async_copy(buffers[k], targets[k], store_sem.at[k]) for k in range(count)
+    ]
+    for load in loads:
+        load.start()
+    for load, store in zip(loads, stores):
+        load.wait()
+        store.start()
+    for store in stores:
+        store.wait()
 
 
 def per_device(
@@ -617,8 +631,10 @@
     return pl.pallas_call(
         hand_on,
         out_shape=[jax.ShapeDtypeStruct(shape, F32) for shape in outputs.values()],
-        in_specs=[pl.BlockSpec(memory_space=pltpu.VMEM)] * len(outputs),
-        out_specs=[pl.BlockSpec(memory_space=pltpu.VMEM)] * len(outputs),
+        in_specs=[pl.BlockSpec(memory_space=pl.ANY)] * len(outputs),
+        out_specs=[pl.BlockSpec(memory_space=pl.ANY)] * len(outputs),
+        scratch_shapes=[pltpu.VMEM(shape, F32) for shape in outputs.values()]
+        + [pltpu.SemaphoreType.DMA((len(outputs),))] * 2,
     )(*results)
 
 

time: 134 us -> 128 us (0.955)
  Pallas kernels: 133 us -> 127 us
    pallas_call x1, Pallas kernels: 130 us -> 124 us  [per_device(): pl.pallas_call(functools.partial(kernel, n_z, n_x, n_y, names), out_shape...]
where the time goes in v4:
time: 128 us
  Pallas kernels  127 us (99%)
    pallas_call x1, Pallas kernels, per_device(): pl.pallas_call(functools.partial(kernel, n_z, n_x, n_y, names), out_shape...  124 us
    pallas_call x1, Pallas kernels, per_device(): pl.pallas_call(hand_on, out_shape=[jax.ShapeDtypeStruct(shape, F32) for s...  2.85 us

profile of v4, /device:TPU:1, one launch (start us, length us, event | category | flops | bytes accessed | tf_op | source)
XLA Modules:
  0.0 127.8 jit_solution(5211942558831214185)
XLA Ops:
  0.6 124.3 %shard_map.120 = (f32[32,4096]{1,0:T(8,128)}, f32[64,1024]{1,0:T(8,128)}, f32[1024,256]{1,0:T(8,128)}, f32[1024,256]{1,0:T(8,128)}) custom-call(bf16[32,4096]{1,0:T(8,128)(2,1)} %refs_0_.1, bf16[4096,1024]{1,0:T(8,128)(2,1)} %refs_1_.1, bf16[1024,256]{1,0:T(8,128)(2,1)} %refs_2_.1, bf16[1024,256]{1,0:T(8,128)(2,1)} %refs_3_.1, bf16[256,128]{1,0:T(8,128)(2,1)} %refs_4_.1, ...), custom_call_target="tpu_custom_call" | custom-call | tf_op jit(solution)/shard_map/pallas_call | solution.py:621
  124.9 2.9 %shard_map.121 = (f32[32,4096]{1,0:T(8,128)}, f32[64,1024]{1,0:T(8,128)}, f32[1024,256]{1,0:T(8,128)}, f32[1024,256]{1,0:T(8,128)}) custom-call(f32[32,4096]{1,0:T(8,128)} %get-tuple-element.8.refs_0_, f32[64,1024]{1,0:T(8,128)} %get-tuple-element.9.refs_1_, f32[1024,256]{1,0:T(8,128)} %get-tuple-element.10.refs_2_, f32[1024,256]{1,0:T(8,128)} %get-tuple-element.11.refs_3_), custom_call_target="tpu_custom_call" | custom-call | tf_op jit(solution)/shard_map/pallas_call | solution.py:631

commit v5 on v4

--- a/solution.py
+++ b/solution.py
@@ -60,7 +60,8 @@
 
 def kernel(n_z, n_x, n_y, names, *refs):
     r = dict(zip(names, refs))
-    feats, w_hbm, w_embed, items = r["feats"], r["w_hidden"], r["w_embed"], r["items"]
+    feats, w_hbm = r["feats"], r["w_hidden"]
+    w_embed, items = r["w_embed_v"], r["items_v"]
     n_a, n_b = n_x * n_y, n_z * 2
     rows = n_a * n_b * CAP
     q_dev, depth = feats.shape
@@ -126,8 +127,6 @@
         whole(stage, group, target).wait_recv()
 
     weights = r["weights"]
-    load = pltpu.make_async_copy(w_hbm, weights, r["load_sem"])
-    load.start()
     barrier = pltpu.get_barrier_semaphore()
     for group in ("a", "b"):
         each(
@@ -137,7 +136,19 @@
             ),
         )
     feats_y = r["feats_y"]
-    feats_y[y] = feats[...]
+    loads = [
+        pltpu.make_async_copy(source, target, r["load_sem"].at[k])
+        for k, (source, target) in enumerate(
+            (
+                (feats, feats_y.at[y]),
+                (w_hbm, weights),
+                (r["w_embed"], w_embed),
+                (r["items"], items),
+            )
+        )
+    ]
+    for load in loads:
+        load.start()
 
     perm = r["perm"]
     log_a, log_b = n_a.bit_length() - 1, n_b.bit_length() - 1
@@ -227,7 +238,8 @@
     second("e1", False)
 
     receive("feats", "y", lambda p: feats_y.at[p])
-    load.wait()
+    for load in loads:
+        load.wait()
     preact, preact_x = r["preact"], r["preact_x"]
     group_rows = n_y * q_dev
     everyone = feats_y[...].reshape(group_rows, depth)
@@ -495,22 +507,31 @@
 
     def item_block(j, carry):
         columns = pl.ds(pl.multiple_of(j * 256, 256), 256)
-        r["grad_items"][columns, :] = tn(
+        r["items_o"][columns, :] = tn(
             spread[:, columns], queries[...].reshape(rows, emb)
         )
         return carry
 
     lax.fori_loop(0, BLK_DEV * BLK // 256, item_block, 0)
+    stores = [
+        pltpu.make_async_copy(r[name + "_o"], r["grad_" + name], r["store_sem"].at[k])
+        for k, name in enumerate(("items", "feats", "embed"))
+    ]
+    stores[0].start()
     for part in range(4):
         columns = pl.ds(part * (depth // 4), depth // 4)
         receive("gf" + str(part), "y", lambda p: gf_r.at[p, :, columns])
     gf_r[y] = gf_s[y]
-    r["grad_feats"][...] = jnp.sum(gf_r[...].astype(F32), axis=0)
+    r["feats_o"][...] = jnp.sum(gf_r[...].astype(F32), axis=0)
+    stores[1].start()
     receive("ex", "x", lambda p: ex.at[p])
-    r["grad_embed"][...] = ex[...].astype(F32).reshape(units, emb)
+    r["embed_o"][...] = ex[...].astype(F32).reshape(units, emb)
+    stores[2].start()
     receive("zs", "z", lambda p: z_r.at[p])
     z_r[z] = jnp.zeros((half, units), BF16)
     r["grad_hidden"][...] = own + jnp.sum(z_r[...].astype(F32), axis=0)
+    for store in stores:
+        store.wait()
     for finish in pending:
         finish()
 
@@ -566,6 +587,11 @@
     }
     vmem = {
         "weights": ((depth, units), BF16),
+        "w_embed_v": ((units, emb), BF16),
+        "items_v": ((BLK_DEV * BLK, emb), BF16),
+        "items_o": ((BLK_DEV * BLK, emb), F32),
+        "feats_o": ((q_dev, depth), F32),
+        "embed_o": ((units, emb), F32),
         "feats_y": ((n_y, q_dev, depth), BF16),
         "perm": ((rows, rows), BF16),
         "member_row": ((rows, q_dev), F32),
@@ -611,18 +637,23 @@
     scratch += [
         pltpu.SemaphoreType.DMA((len(STAGES), most)),
         pltpu.SemaphoreType.DMA((len(STAGES), most)),
-        pltpu.SemaphoreType.DMA,
+        pltpu.SemaphoreType.DMA((4,)),
+        pltpu.SemaphoreType.DMA((3,)),
     ]
-    names = list(inputs) + list(outputs) + list(vmem) + ["send_sem", "recv_sem", "load_sem"]
+    names = list(inputs) + list(outputs) + list(vmem) + ["send_sem", "recv_sem", "load_sem", "store_sem"]
+    large = ("feats", "w_hidden", "w_embed", "items")
     specs = [
-        pl.BlockSpec(memory_space=pl.ANY if name == "w_hidden" else pltpu.VMEM)
+        pl.BlockSpec(memory_space=pl.ANY if name in large else pltpu.VMEM)
         for name in inputs
     ]
     results = pl.pallas_call(
         functools.partial(kernel, n_z, n_x, n_y, names),
         out_shape=[jax.ShapeDtypeStruct(shape, F32) for shape in outputs.values()],
         in_specs=specs,
-        out_specs=[pl.BlockSpec(memory_space=pltpu.VMEM)] * len(outputs),
+        out_specs=[
+            pl.BlockSpec(memory_space=pltpu.VMEM if name == "grad_hidden" else pl.ANY)
+            for name in outputs
+        ],
         scratch_shapes=scratch,
         compiler_params=pltpu.CompilerParams(
             collective_id=0, has_side_effects=True, vmem_limit_bytes=58 * 1024 * 1024

time: 128 us -> 127 us (level)
  no operation moved by 1% of the time
where the time goes in v5:
time: 127 us
  Pallas kernels  126 us (99%)
    pallas_call x1, Pallas kernels, per_device(): pl.pallas_call(functools.partial(kernel, n_z, n_x, n_y, names), out_shape...  123 us
    pallas_call x1, Pallas kernels, per_device(): pl.pallas_call(hand_on, out_shape=[jax.ShapeDtypeStruct(shape, F32) for s...  2.85 us

profile of v5, /device:TPU:1, one launch (start us, length us, event | category | flops | bytes accessed | tf_op | source)
XLA Modules:
  0.0 127.0 jit_solution(11505392970884628875)
XLA Ops:
  0.6 123.5 %shard_map.120 = (f32[32,4096]{1,0:T(8,128)}, f32[64,1024]{1,0:T(8,128)}, f32[1024,256]{1,0:T(8,128)}, f32[1024,256]{1,0:T(8,128)}) custom-call(bf16[32,4096]{1,0:T(8,128)(2,1)} %refs_0_.1, bf16[4096,1024]{1,0:T(8,128)(2,1)} %refs_1_.1, bf16[1024,256]{1,0:T(8,128)(2,1)} %refs_2_.1, bf16[1024,256]{1,0:T(8,128)(2,1)} %refs_3_.1, bf16[256,128]{1,0:T(8,128)(2,1)} %refs_4_.1, ...), custom_call_target="tpu_custom_call" | custom-call | tf_op jit(solution)/shard_map/pallas_call | solution.py:649
  124.1 2.9 %shard_map.121 = (f32[32,4096]{1,0:T(8,128)}, f32[64,1024]{1,0:T(8,128)}, f32[1024,256]{1,0:T(8,128)}, f32[1024,256]{1,0:T(8,128)}) custom-call(f32[32,4096]{1,0:T(8,128)} %get-tuple-element.8.refs_0_, f32[64,1024]{1,0:T(8,128)} %get-tuple-element.9.refs_1_, f32[1024,256]{1,0:T(8,128)} %get-tuple-element.10.refs_2_, f32[1024,256]{1,0:T(8,128)} %get-tuple-element.11.refs_3_), custom_call_target="tpu_custom_call" | custom-call | tf_op jit(solution)/shard_map/pallas_call | solution.py:662
